TPU v7x, 32 devices: a whole 2x2x4 slice. The times are simulated.
32 devices in a mesh: tower: 2 (over x), dp: 16 (over z, y, core).
Axes of the slice: x: 2, y: 2, z: 4, core: 2. Of those that a mesh axis runs over, the one named last changes fastest.
Arguments:
- tokens: bfloat16 [2, 3072, 768], P('tower', 'dp'), may hold values from -21 to 21
- cotangent: bfloat16 [2, 3072, 768], P('tower', 'dp'), may hold values from -6 to 6
- kept_counts: int32 [16, 3], P('dp'), may hold values from 1 to 144, 192 in all within a row
- caption_lengths: int32 [48], P('dp'), may hold values from 16 to 64
- attn_gain: bfloat16 [2, 768], P('tower', 'dp'), may hold values from 0.5 to 1.5
- qkv_weight: bfloat16 [2, 768, 2304], P('tower', 'dp'), may hold values from -0.21875 to 0.21875
- attn_out: bfloat16 [2, 768, 768], P('tower', 'dp'), may hold values from -0.875 to 0.875
- mlp_gain: bfloat16 [2, 768], P('tower', 'dp'), may hold values from 0.5 to 1.5
- mlp_up: bfloat16 [2, 768, 3072], P('tower', 'dp'), may hold values from -0.21875 to 0.21875
- mlp_down: bfloat16 [2, 3072, 768], P('tower', 'dp'), may hold values from -0.109375 to 0.109375
- query_gain: bfloat16 [768], P(('tower', 'dp')), may hold values from 0.5 to 1.5
- image_gain: bfloat16 [768], P(('tower', 'dp')), may hold values from 0.5 to 1.5
- cross_gain: bfloat16 [768], P(('tower', 'dp')), may hold values from 0.5 to 1.5
- cross_query: bfloat16 [768, 768], P(('tower', 'dp')), may hold values from -0.21875 to 0.21875
- cross_keyval: bfloat16 [768, 1536], P(('tower', 'dp')), may hold values from -0.21875 to 0.21875
- cross_out: bfloat16 [768, 768], P(('tower', 'dp')), may hold values from -0.875 to 0.875
- cross_up: bfloat16 [768, 3072], P(('tower', 'dp')), may hold values from -0.21875 to 0.21875
- cross_down: bfloat16 [3072, 768], P(('tower', 'dp')), may hold values from -0.109375 to 0.109375
Outputs:
- layer_out: bfloat16 [2, 3072, 768], P('tower', 'dp')
- input_grad: float32 [2, 3072, 768], P('tower', 'dp')
- attn_gain_grad: float32 [2, 768], P('tower', 'dp')
- qkv_weight_grad: float32 [2, 768, 2304], P('tower', 'dp')
- attn_out_grad: float32 [2, 768, 768], P('tower', 'dp')
- mlp_gain_grad: float32 [2, 768], P('tower', 'dp')
- mlp_up_grad: float32 [2, 768, 3072], P('tower', 'dp')
- mlp_down_grad: float32 [2, 3072, 768], P('tower', 'dp')
- query_gain_grad: float32 [768], P(('tower', 'dp'))
- image_gain_grad: float32 [768], P(('tower', 'dp'))
- cross_gain_grad: float32 [768], P(('tower', 'dp'))
- cross_query_grad: float32 [768, 768], P(('tower', 'dp'))
- cross_keyval_grad: float32 [768, 1536], P(('tower', 'dp'))
- cross_out_grad: float32 [768, 768], P(('tower', 'dp'))
- cross_up_grad: float32 [768, 3072], P(('tower', 'dp'))
- cross_down_grad: float32 [3072, 768], P(('tower', 'dp'))
- rms_values: float32 [10], replicated
Inputs may be any that keep to these rules, and one draw needn't show every extreme that they name: `kept_counts`: the 3 images of one device keep 192 patches together, one image after another.
All inputs are finite; a program needn't handle non-finite values.
Results may differ from a plain program's by a relative error of at most 0.019.
Values may be sent and summed in bfloat16 or wider, within the bound.
A program may use at most 256 MiB of HBM per device.

v0:
```python
import jax
import jax.numpy as jnp
from jax import lax
from jax.sharding import PartitionSpec as P

HD = 64
CAP_LEN = 64


EPSILON = 1e-06
NEGATIVE = -1000000000.0


def from_behind(block, axis, distance):
    devices = range(lax.axis_size(axis))
    route = [(i - distance, i) for i in devices if i - distance in devices]
    return lax.ppermute(block, axis, route)


def layer_norm(value_matrix, norm_gain):
    center = value_matrix - jnp.mean(value_matrix, axis=-1, keepdims=True)
    spread = jnp.mean(center * center, axis=-1, keepdims=True)
    return center * lax.rsqrt(spread + EPSILON) * norm_gain


def norm_back(value_matrix, norm_gain, grad_out):
    result, puller = jax.vjp(layer_norm, value_matrix, norm_gain)
    return puller(grad_out)


def positions(counts, lengths, row_count):
    row_index = jnp.arange(row_count, dtype=jnp.int32)
    bounds = jnp.cumsum(counts)
    image_of = jnp.sum((row_index[:, None] >= bounds[None, :]).astype(jnp.int32), axis=1)
    caption_of = row_index // CAP_LEN
    in_place = row_index - caption_of * CAP_LEN
    caption_slots = jnp.arange(lengths.shape[0], dtype=jnp.int32)
    length_rows = jnp.sum(
        jnp.where(caption_of[:, None] == caption_slots[None, :], lengths[None, :], 0), axis=1
    )
    valid_rows = in_place < length_rows
    encoder_mask = (image_of[:, None] == image_of[None, :])[None]
    slot_place = jnp.arange(CAP_LEN, dtype=jnp.int32)
    text_blocks = (slot_place[None, None, :] <= slot_place[None, :, None]) & (
        slot_place[None, None, :] < lengths[:, None, None]
    )
    cross_mask = (caption_of[:, None] == image_of[None, :])[None]
    return (encoder_mask, text_blocks, cross_mask, valid_rows)


def by_heads(value_matrix):
    return value_matrix.reshape(value_matrix.shape[0], -1, HD).transpose(1, 0, 2)


def from_heads(value_matrix):
    return value_matrix.transpose(1, 0, 2).reshape(value_matrix.shape[1], -1)


def grouped(value_matrix, group):
    heads = by_heads(value_matrix)
    return heads.reshape(heads.shape[0], -1, group, HD)


def head_scores(head_queries, head_keys, allowed):
    scores = jnp.einsum(
        "jmh,jih->jmi", head_queries, head_keys, preferred_element_type=jnp.float32
    ) * HD ** (-0.5)
    return jnp.where(allowed, scores, NEGATIVE)


def attend(query_rows, key_rows, value_rows, allowed, group):

    def one_head(head_parts):
        head_queries, head_keys, head_values = head_parts
        scores = head_scores(head_queries, head_keys, allowed)
        highest = jnp.max(scores, axis=-1, keepdims=True)
        exponent = jnp.exp(scores - highest)
        totals = jnp.sum(exponent, axis=-1, keepdims=True)
        attention_weight = (exponent / totals).astype(jnp.bfloat16)
        mixture = jnp.einsum(
            "irv,ivg->irg", attention_weight, head_values, preferred_element_type=jnp.float32
        )
        return (mixture.reshape(-1, HD), (highest[..., 0] + jnp.log(totals[..., 0])).reshape(-1))

    mixture, log_total = lax.map(
        one_head, (grouped(query_rows, group), grouped(key_rows, group), grouped(value_rows, group))
    )
    return (from_heads(mixture).astype(jnp.bfloat16), log_total)


def attend_back(query_rows, key_rows, value_rows, allowed, group, log_total, mixture_gradient):

    def one_head(head_parts):
        head_queries, head_keys, head_values, head_total, head_gradient = head_parts
        scores = head_scores(head_queries, head_keys, allowed)
        attention_weight = jnp.exp(scores - head_total.reshape(-1, group)[:, :, None])
        grad_value = jnp.einsum(
            "cmg,cmo->cgo",
            attention_weight.astype(jnp.bfloat16),
            head_gradient,
            preferred_element_type=jnp.float32,
        )
        grad_weights = jnp.einsum(
            "jmh,jih->jmi", head_gradient, head_values, preferred_element_type=jnp.float32
        )
        score_gradient = attention_weight * (
            grad_weights - jnp.sum(grad_weights * attention_weight, axis=-1, keepdims=True)
        )
        score_gradient = score_gradient.astype(jnp.bfloat16)
        grad_query = jnp.einsum(
            "irv,ivg->irg", score_gradient, head_keys, preferred_element_type=jnp.float32
        ) * HD ** (-0.5)
        grad_key = jnp.einsum(
            "cmg,cmo->cgo", score_gradient, head_queries, preferred_element_type=jnp.float32
        ) * HD ** (-0.5)
        return (grad_query.reshape(-1, HD), grad_key.reshape(-1, HD), grad_value.reshape(-1, HD))

    head_parts = (
        grouped(query_rows, group),
        grouped(key_rows, group),
        grouped(value_rows, group),
        log_total,
        grouped(mixture_gradient, group),
    )
    grad_query, grad_key, grad_value = lax.map(one_head, head_parts)
    return (from_heads(grad_query), from_heads(grad_key), from_heads(grad_value))


def mlp_forward(stream, norm_gain, up_weight, down_weight):
    hidden_in = layer_norm(stream, norm_gain.astype(jnp.float32)).astype(jnp.bfloat16)
    up_value = jnp.dot(hidden_in, up_weight, preferred_element_type=jnp.float32)
    active = jax.nn.gelu(up_value).astype(jnp.bfloat16)
    branch = jnp.dot(active, down_weight, preferred_element_type=jnp.float32)
    return (branch, (hidden_in, up_value, active))


def mlp_back(stream, norm_gain, up_weight, down_weight, stored, grad_out):
    hidden_in, up_value, active = stored
    grad_branch = grad_out.astype(jnp.bfloat16)
    grad_down = jnp.einsum("rf,rd->fd", active, grad_branch, preferred_element_type=jnp.float32)
    grad_active = jnp.einsum(
        "rd,fd->rf", grad_branch, down_weight, preferred_element_type=jnp.float32
    )
    result, puller = jax.vjp(jax.nn.gelu, up_value)
    grad_up_value = puller(grad_active)[0].astype(jnp.bfloat16)
    grad_up = jnp.einsum("rd,rf->df", hidden_in, grad_up_value, preferred_element_type=jnp.float32)
    grad_hidden = jnp.einsum(
        "rf,df->rd", grad_up_value, up_weight, preferred_element_type=jnp.float32
    )
    grad_stream, grad_gain = norm_back(stream, norm_gain.astype(jnp.float32), grad_hidden)
    return (grad_out + grad_stream, grad_gain, grad_up, grad_down)


def self_forward(stream, attention_weight, allowed, group):
    attn_gain, qkv_weight, attn_out, mlp_gain, mlp_up, mlp_down = attention_weight
    normed = layer_norm(stream, attn_gain.astype(jnp.float32)).astype(jnp.bfloat16)
    joined = jnp.dot(normed, qkv_weight, preferred_element_type=jnp.float32).astype(jnp.bfloat16)
    query_rows, key_rows, value_rows = jnp.split(joined, 3, axis=1)
    mixture, log_total = attend(query_rows, key_rows, value_rows, allowed, group)
    attn_branch = jnp.dot(mixture, attn_out, preferred_element_type=jnp.float32)
    middle = stream + attn_branch
    mlp_branch, mlp_stored = mlp_forward(middle, mlp_gain, mlp_up, mlp_down)
    return (
        middle + mlp_branch,
        (normed, joined, mixture, log_total, middle, mlp_stored),
        (attn_branch, mlp_branch),
    )


def self_back(stream, attention_weight, allowed, group, stored, grad_out):
    attn_gain, qkv_weight, attn_out, mlp_gain, mlp_up, mlp_down = attention_weight
    normed, joined, mixture, log_total, middle, mlp_stored = stored
    grad_middle, grad_mlp_gain, grad_up, grad_down = mlp_back(
        middle, mlp_gain, mlp_up, mlp_down, mlp_stored, grad_out
    )
    grad_branch = grad_middle.astype(jnp.bfloat16)
    grad_attn_out = jnp.einsum(
        "re,rd->ed", mixture, grad_branch, preferred_element_type=jnp.float32
    )
    mixture_gradient = jnp.einsum(
        "rd,ed->re", grad_branch, attn_out, preferred_element_type=jnp.float32
    ).astype(jnp.bfloat16)
    query_rows, key_rows, value_rows = jnp.split(joined, 3, axis=1)
    grad_parts = attend_back(
        query_rows, key_rows, value_rows, allowed, group, log_total, mixture_gradient
    )
    grad_joined = jnp.concatenate(grad_parts, axis=1).astype(jnp.bfloat16)
    grad_qkv = jnp.einsum("rd,re->de", normed, grad_joined, preferred_element_type=jnp.float32)
    grad_normed = jnp.einsum(
        "re,de->rd", grad_joined, qkv_weight, preferred_element_type=jnp.float32
    )
    grad_stream, grad_attn_gain = norm_back(stream, attn_gain.astype(jnp.float32), grad_normed)
    return (
        grad_middle + grad_stream,
        (grad_attn_gain, grad_qkv, grad_attn_out, grad_mlp_gain, grad_up, grad_down),
    )


def project_keyval(image_rows, attention_weight):
    normed = layer_norm(
        image_rows.astype(jnp.float32), attention_weight[1].astype(jnp.float32)
    ).astype(jnp.bfloat16)
    keyval = jnp.dot(normed, attention_weight[4], preferred_element_type=jnp.float32).astype(
        jnp.bfloat16
    )
    return (keyval, normed)


def keyval_back(image_rows, attention_weight, normed, grad_keyval):
    grad_weight = jnp.einsum("rd,re->de", normed, grad_keyval, preferred_element_type=jnp.float32)
    grad_normed = jnp.einsum(
        "re,de->rd", grad_keyval, attention_weight[4], preferred_element_type=jnp.float32
    )
    grad_image, grad_gain = norm_back(
        image_rows.astype(jnp.float32), attention_weight[1].astype(jnp.float32), grad_normed
    )
    return (grad_image, grad_gain, grad_weight)


def cross_forward(stream, keyval, attention_weight, allowed):
    normed = layer_norm(stream, attention_weight[0].astype(jnp.float32)).astype(jnp.bfloat16)
    query_rows = jnp.dot(normed, attention_weight[3], preferred_element_type=jnp.float32).astype(
        jnp.bfloat16
    )
    key_rows, value_rows = jnp.split(keyval, 2, axis=1)
    mixture, log_total = attend(query_rows, key_rows, value_rows, allowed, stream.shape[0])
    attn_branch = jnp.dot(mixture, attention_weight[5], preferred_element_type=jnp.float32)
    middle = stream + attn_branch
    mlp_branch, mlp_stored = mlp_forward(
        middle, attention_weight[2], attention_weight[6], attention_weight[7]
    )
    return (
        middle + mlp_branch,
        (normed, query_rows, mixture, log_total, middle, mlp_stored),
        (attn_branch, mlp_branch),
    )


def cross_back(stream, keyval, attention_weight, allowed, stored, grad_out):
    normed, query_rows, mixture, log_total, middle, mlp_stored = stored
    grad_middle, grad_mlp_gain, grad_up, grad_down = mlp_back(
        middle, attention_weight[2], attention_weight[6], attention_weight[7], mlp_stored, grad_out
    )
    grad_branch = grad_middle.astype(jnp.bfloat16)
    grad_cross_out = jnp.einsum(
        "re,rd->ed", mixture, grad_branch, preferred_element_type=jnp.float32
    )
    mixture_gradient = jnp.einsum(
        "rd,ed->re", grad_branch, attention_weight[5], preferred_element_type=jnp.float32
    ).astype(jnp.bfloat16)
    key_rows, value_rows = jnp.split(keyval, 2, axis=1)
    grad_query, grad_key, grad_value = attend_back(
        query_rows, key_rows, value_rows, allowed, stream.shape[0], log_total, mixture_gradient
    )
    grad_query = grad_query.astype(jnp.bfloat16)
    grad_query_weight = jnp.einsum(
        "rd,re->de", normed, grad_query, preferred_element_type=jnp.float32
    )
    grad_normed = jnp.einsum(
        "re,de->rd", grad_query, attention_weight[3], preferred_element_type=jnp.float32
    )
    grad_stream, grad_query_gain = norm_back(
        stream, attention_weight[0].astype(jnp.float32), grad_normed
    )
    grad_keyval = jnp.concatenate([grad_key, grad_value], axis=1).astype(jnp.bfloat16)
    six_grads = (
        grad_query_gain,
        grad_mlp_gain,
        grad_query_weight,
        grad_cross_out,
        grad_up,
        grad_down,
    )
    return (grad_middle + grad_stream, grad_keyval, six_grads)


def assemble(six_grads, gain_grad, weight_grad):
    return (
        six_grads[0],
        gain_grad,
        six_grads[1],
        six_grads[2],
        weight_grad,
        six_grads[3],
        six_grads[4],
        six_grads[5],
    )


def squares(value_matrix, row_weight):
    return jnp.sum(row_weight[:, None] * value_matrix * value_matrix)


def shards(
    tokens,
    cotangent,
    kept_counts,
    caption_lengths,
    attn_gain,
    qkv_weight,
    attn_out,
    mlp_gain,
    mlp_up,
    mlp_down,
    query_gain,
    image_gain,
    cross_gain,
    cross_query,
    cross_keyval,
    cross_out,
    cross_up,
    cross_down,
):
    gathered = (
        lax.all_gather(attn_gain, "dp", axis=1, tiled=True),
        lax.all_gather(qkv_weight, "dp", axis=1, tiled=True),
        lax.all_gather(attn_out, "dp", axis=1, tiled=True),
        lax.all_gather(mlp_gain, "dp", axis=1, tiled=True),
        lax.all_gather(mlp_up, "dp", axis=1, tiled=True),
        lax.all_gather(mlp_down, "dp", axis=1, tiled=True),
    )
    layer_weights = tuple((member[0] for member in gathered))
    cross_weights = (
        lax.all_gather(query_gain, ("tower", "dp"), axis=0, tiled=True),
        lax.all_gather(image_gain, ("tower", "dp"), axis=0, tiled=True),
        lax.all_gather(cross_gain, ("tower", "dp"), axis=0, tiled=True),
        lax.all_gather(cross_query, ("tower", "dp"), axis=0, tiled=True),
        lax.all_gather(cross_keyval, ("tower", "dp"), axis=0, tiled=True),
        lax.all_gather(cross_out, ("tower", "dp"), axis=0, tiled=True),
        lax.all_gather(cross_up, ("tower", "dp"), axis=0, tiled=True),
        lax.all_gather(cross_down, ("tower", "dp"), axis=0, tiled=True),
    )
    decoder = lax.axis_index("tower") == 1
    row_count = tokens.shape[1]
    width = tokens.shape[2]
    stream = tokens[0].astype(jnp.float32)
    upstream = cotangent[0].astype(jnp.float32)
    encoder_mask, text_blocks, cross_mask, valid_rows = positions(
        kept_counts[0], caption_lengths, row_count
    )
    row_weight = jnp.where(decoder, valid_rows, True).astype(jnp.float32)

    def text_forward(value_matrix):
        return self_forward(value_matrix, layer_weights, text_blocks, CAP_LEN)

    def image_forward(value_matrix):
        return self_forward(value_matrix, layer_weights, encoder_mask, row_count)

    layer_y, layer_stored, layer_branches = lax.cond(decoder, text_forward, image_forward, stream)
    image_rows = layer_y.astype(jnp.bfloat16)
    blank_rows = jnp.zeros((row_count, width), jnp.float32)
    blank_grads = tuple((jnp.zeros(member.shape, jnp.float32) for member in cross_weights))
    blank_sums = jnp.zeros((3,), jnp.float32)
    arrived = from_behind(image_rows, "tower", 1)

    def run_cross(operands):
        text_y, image_in = operands
        keyval, normed = project_keyval(image_in, cross_weights)
        final_rows, stored, branches = cross_forward(text_y, keyval, cross_weights, cross_mask)
        grad_text, grad_keyval, six_grads = cross_back(
            text_y, keyval, cross_weights, cross_mask, stored, upstream
        )
        grad_image, grad_gain, grad_weight = keyval_back(
            image_in, cross_weights, normed, grad_keyval
        )
        cross_sums = jnp.stack(
            [
                squares(branches[0], row_weight),
                squares(branches[1], row_weight),
                squares(final_rows, row_weight),
            ]
        )
        return (
            final_rows,
            grad_text,
            grad_image,
            assemble(six_grads, grad_gain, grad_weight),
            cross_sums,
        )

    def skip_cross(operands):
        return (blank_rows, blank_rows, blank_rows, blank_grads, blank_sums)

    final_rows, grad_text, grad_image, cross_grads, cross_sums = lax.cond(
        decoder, run_cross, skip_cross, (layer_y, arrived)
    )
    returned = from_behind(grad_image.astype(jnp.bfloat16), "tower", -1).astype(grad_image.dtype)
    grad_top = jnp.where(decoder, grad_text, upstream + returned)

    def text_backward(operands):
        return self_back(operands[0], layer_weights, text_blocks, CAP_LEN, operands[1], operands[2])

    def image_backward(operands):
        return self_back(
            operands[0], layer_weights, encoder_mask, row_count, operands[1], operands[2]
        )

    grad_stream, layer_grads = lax.cond(
        decoder, text_backward, image_backward, (stream, layer_stored, grad_top)
    )
    dp_count = lax.axis_size("dp")
    group_count = lax.axis_size("tower") * dp_count
    layer_flat = lax.psum_scatter(
        tuple((member.reshape(-1) for member in layer_grads)), "dp", scatter_dimension=0, tiled=True
    )
    layer_shards = tuple(
        (
            piece.reshape((1, member.shape[0] // dp_count) + member.shape[1:])
            for piece, member in zip(layer_flat, layer_grads)
        )
    )
    cross_flat = lax.psum_scatter(
        tuple((member.reshape(-1) for member in cross_grads)),
        ("tower", "dp"),
        scatter_dimension=0,
        tiled=True,
    )
    cross_shards = tuple(
        (
            piece.reshape((member.shape[0] // group_count,) + member.shape[1:])
            for piece, member in zip(cross_flat, cross_grads)
        )
    )
    attn_branch, mlp_branch = layer_branches
    layer_sums = jnp.stack(
        [
            squares(stream, row_weight),
            squares(attn_branch, row_weight),
            squares(mlp_branch, row_weight),
            squares(layer_y, row_weight),
        ]
    )
    encoder_part = jnp.where(decoder, 0.0, layer_sums)
    decoder_part = jnp.where(decoder, jnp.concatenate([layer_sums[:3], cross_sums]), 0.0)
    counted = jnp.where(decoder, jnp.sum(valid_rows.astype(jnp.float32)), 0.0)
    totals, counted_all = lax.psum(
        (jnp.concatenate([encoder_part, decoder_part]), counted), ("tower", "dp")
    )
    encoder_count = float(row_count * dp_count)
    divisor = (
        jnp.concatenate(
            [
                jnp.full((4,), encoder_count, jnp.float32),
                jnp.full((6,), 1.0, jnp.float32) * counted_all,
            ]
        )
        * width
    )
    rms_values = jnp.sqrt(totals / divisor)
    layer_out = jnp.where(decoder, final_rows, layer_y).astype(jnp.bfloat16)
    return (
        layer_out[None],
        grad_stream[None],
        layer_shards[0],
        layer_shards[1],
        layer_shards[2],
        layer_shards[3],
        layer_shards[4],
        layer_shards[5],
        cross_shards[0],
        cross_shards[1],
        cross_shards[2],
        cross_shards[3],
        cross_shards[4],
        cross_shards[5],
        cross_shards[6],
        cross_shards[7],
        rms_values,
    )


def solution(mesh):
    placed = (
        P("tower", "dp", None),
        P("tower", "dp", None),
        P("dp", None),
        P("dp"),
        P("tower", "dp"),
        P("tower", "dp", None),
        P("tower", "dp", None),
        P("tower", "dp"),
        P("tower", "dp", None),
        P("tower", "dp", None),
        P(("tower", "dp")),
        P(("tower", "dp")),
        P(("tower", "dp")),
        P(("tower", "dp"), None),
        P(("tower", "dp"), None),
        P(("tower", "dp"), None),
        P(("tower", "dp"), None),
        P(("tower", "dp"), None),
    )
    return jax.shard_map(
        shards,
        mesh=mesh,
        in_specs=placed,
        out_specs=(
            P("tower", "dp", None),
            P("tower", "dp", None),
            P("tower", "dp"),
            P("tower", "dp", None),
            P("tower", "dp", None),
            P("tower", "dp"),
            P("tower", "dp", None),
            P("tower", "dp", None),
            P(("tower", "dp")),
            P(("tower", "dp")),
            P(("tower", "dp")),
            P(("tower", "dp"), None),
            P(("tower", "dp"), None),
            P(("tower", "dp"), None),
            P(("tower", "dp"), None),
            P(("tower", "dp"), None),
            P(),
        ),
        check_vma=False,
    )
```

profile of v0, /device:TPU:0, one launch (start us, length us, event | category | flops | bytes accessed | tf_op | source)
XLA Modules:
  0.0 1655.6 jit_solution(5158109561436654577)
XLA Ops:
  17.9 35.2 %all-reduce.25 = (bf16[768]{0:T(1024)(128)(2,1)S(1)}, bf16[768]{0:T(1024)(128)(2,1)S(1)}) all-reduce(bf16[768]{0:T(1024)(128)(2,1)S(1)} %dynamic-update-slice, bf16[768]{0:T(1024)(128)(2,1)S(1)} %dynamic-update-slice.1), channel_id=1, replica_groups=mesh['tower'=2,'dp'=16] {'dp'}, use_global_device_ids=true, to_apply=%add.1 | all-reduce | flops 1536 | bytes 6144 | tf_op jit(solution)/shard_map/squeeze | solution.py:322
  56.5 43.5 %all-gather.10.cloned.1.call-done = bf16[1,768,2304]{2,1,0:T(8,128)(2,1)} async-done(((bf16[1,48,2304]{2,1,0:T(8,128)(2,1)}), bf16[1,768,2304]{2,1,0:T(8,128)(2,1)}) %all-gather.10.cloned.1.call-update) | async-done | bytes 3538960 | tf_op jit(solution)/shard_map/all_gather | solution.py:316
  100.0 54.7 %all-gather.14.cloned.1.call-done = bf16[1,768,3072]{2,1,0:T(8,128)(2,1)} async-done(((bf16[1,48,3072]{2,1,0:T(8,128)(2,1)}), bf16[1,768,3072]{2,1,0:T(8,128)(2,1)}) %all-gather.14.cloned.1.call-update) | async-done | bytes 4718608 | tf_op jit(solution)/shard_map/all_gather | solution.py:319
  154.7 54.1 %all-gather.16.cloned.1.call-done = bf16[1,3072,768]{2,1,0:T(8,128)(2,1)} async-done(((bf16[1,192,768]{2,1,0:T(8,128)(2,1)}), bf16[1,3072,768]{2,1,0:T(8,128)(2,1)}) %all-gather.16.cloned.1.call-update) | async-done | bytes 4718608 | tf_op jit(solution)/shard_map/all_gather | solution.py:320
  208.9 32.4 %conditional.8 = (bf16[192,2304]{1,0:T(8,128)(2,1)}, f32[12,192]{1,0:T(8,128)S(1)}, f32[192,768]{1,0:T(8,128)S(1)}, f32[192,3072]{1,0:T(8,128)}, f32[192,768]{1,...) conditional(s32[]{:T(128)} %convert_element_type.275, ...), branch_computations={%region_2.11_spmd, %region_11.20_spmd} | conditional | flops 2735458048 | bytes 81289240
  214.7 16.5 while.90
  244.4 39.3 %collective-permute-start = (bf16[192,768]{1,0:T(8,128)(2,1)S(1)}, bf16[192,768]{1,0:T(8,128)(2,1)S(1)}, u32[]{:S(2)}, u32[]{:S(2)}) collective-permute-start(bf16[192,768]{1,0:T(8,128)(2,1)S(1)} %convert_element_type.279), channel_id=1, source_target_pairs={{0,16},{1,17},{2,18},{3,19},{4,20},{5,21},{6,22},{7,23},{8,24},{9,... | collective-permute-start | bytes 884744 | tf_op jit(solution)/shard_map/ppermute | solution.py:17
  284.4 39.8 %all-reduce.24 = (bf16[768]{0:T(1024)(128)(2,1)S(1)}, bf16[768]{0:T(1024)(128)(2,1)S(1)}, bf16[768]{0:T(1024)(128)(2,1)}) all-reduce(bf16[768]{0:T(1024)(128)(2,1)S(1)} %dynamic-update-slice.2, bf16[768]{0:T(1024)(128)(2,1)S(1)} %dynamic-update-slice.3, ...), channel_id=1, replica_groups=mesh['tower'=2,'dp'=16] {'tower','dp'}, use_global_device_ids=true, to_apply=%add.3 | all-reduce | flops 2304 | bytes 9216
  324.3 55.1 %all-gather.20.cloned.1.call-done = bf16[768,1536]{1,0:T(8,128)(2,1)} async-done(((bf16[24,1536]{1,0:T(8,128)(2,1)}), bf16[768,1536]{1,0:T(8,128)(2,1)}) %all-gather.20.cloned.1.call-update) | async-done | bytes 2359312 | tf_op jit(solution)/shard_map/all_gather | solution.py:328
  379.4 65.3 %all-gather.24.cloned.1.call-done = bf16[768,3072]{1,0:T(8,128)(2,1)} async-done(((bf16[24,3072]{1,0:T(8,128)(2,1)}), bf16[768,3072]{1,0:T(8,128)(2,1)}) %all-gather.24.cloned.1.call-update) | async-done | bytes 4718608 | tf_op jit(solution)/shard_map/all_gather | solution.py:330
  444.7 65.3 %all-gather.26.cloned.1.call-done = bf16[3072,768]{1,0:T(8,128)(2,1)} async-done(((bf16[96,768]{1,0:T(8,128)(2,1)}), bf16[3072,768]{1,0:T(8,128)(2,1)}) %all-gather.26.cloned.1.call-update) | async-done | bytes 4718608 | tf_op jit(solution)/shard_map/all_gather | solution.py:331
  510.0 21.7 %conditional.6 = (f32[192,768]{1,0:T(8,128)}, f32[192,768]{1,0:T(8,128)}, f32[192,768]{1,0:T(8,128)}, f32[768]{0:T(1024)S(1)}, f32[768]{0:T(1024)S(1)}, /*index=...) conditional(s32[]{:T(128)} %convert_element_type.275, () %tuple.84, ...), branch_computations={%region_21.22_spmd, %region_22.48_spmd} | conditional | flops 8229179392 | bytes 177606848 | solution.py:384
  531.8 9.5 copy.268
  541.3 10.8 reshape.983
  569.0 161.2 %collective-permute-done.1 = bf16[192,768]{1,0:T(8,128)(2,1)S(1)} collective-permute-done((bf16[192,768]{1,0:T(8,128)(2,1)S(1)}, bf16[192,768]{1,0:T(8,128)(2,1)S(1)}, u32[]{:S(2)}, u32[]{:S(2)}) %collective-permute-start.1) | collective-permute-done | bytes 294944 | tf_op jit(solution)/shard_map/ppermute | solution.py:17
  732.2 107.6 %conditional.7 = (f32[768,2304]{0,1:T(8,128)}, f32[768,768]{0,1:T(8,128)}, f32[768,3072]{0,1:T(8,128)}, f32[3072,768]{1,0:T(8,128)}, f32[192,768]{1,0:T(8,128)S(...) conditional(s32[]{:T(128)} %convert_element_type.275, ...), branch_computations={%region_48.59_spmd, %region_59.70_spmd} | conditional | flops 5482330624 | bytes 92751504 | solution.py:398
  751.4 61.3 %while.94 = (s32[]{:T(128)}, bf16[12,192,64]{1,2,0:T(8,128)(2,1)}, bf16[12,192,64]{1,2,0:T(8,128)(2,1)}, bf16[12,192,64]{1,2,0:T(8,128)(2,1)}, pred[1,192,192]{1...) while((s32[]{:T(128)}, bf16[12,192,64]{1,2,0:T(8,128)(2,1)}, ...), condition=%wide.region_55.55_spmd, body=%wide.region_53.54_spmd.sunk | while | flops 23949120 | bytes 1737841 | solution.py:125
  839.8 9.8 copy.252
  849.7 9.8 copy.267
  875.5 10.8 reshape.973
  901.5 64.2 %all-reduce.20 = (f32[768]{0:T(1024)S(1)}, f32[768]{0:T(1024)S(1)}, f32[768]{0:T(1024)S(1)}, f32[10]{0:T(128)S(1)}, f32[]{:T(128)}) all-reduce(f32[768]{0:T(1024)S(1)} %get-tuple-element.723, f32[768]{0:T(1024)S(1)} %copy-done.47, f32[768]{0:T(1024)S(1)} %copy-done.49, ...), channel_id=8, replica_groups=mesh['tower'=2,'dp'=16] {'tower','dp'}, use_global_device_ids=true, to_apply=%region_79.80.clone | all-reduce | flops 2315 | bytes 18520
  972.2 34.4 %all-reduce.22 = (f32[768]{0:T(1024)S(1)}, f32[768]{0:T(1024)S(1)}) all-reduce(f32[768]{0:T(1024)S(1)} %get-tuple-element.1297, f32[768]{0:T(1024)S(1)} %get-tuple-element.1296), channel_id=2, replica_groups=mesh['tower'=2,'dp'=16] {'dp'}, use_global_device_ids=true, to_apply=%region_72.73.clone | all-reduce | flops 1536 | bytes 12288
  1009.9 139.3 %all-reduce.29.cloned.1.call-done = (f32[589824]{0:T(1024)}, f32[1179648]{0:T(1024)}, f32[589824]{0:T(1024)}, f32[2359296]{0:T(1024)}, f32[2359296]{0:T(1024)}) async-done(((f32[589824]{0:T(1024)}, f32[1179648]{0:T(1024)}, f32[589824]{0:T(1024)}, f32[2359296]{0:T(1024)}, f32[2359296]{0:T(1024)}), (f32[589824]{0:T(1024)}, f32[1179648]{0:T(1024)}, f32[589824]{0:T(1024)}, f32[2359296]{0:T(1024)}, ...) | async-done | bytes 28311568
  1157.5 483.7 %all-reduce.31.cloned.1.call-done = (f32[1769472]{0:T(1024)}, f32[589824]{0:T(1024)}, f32[2359296]{0:T(1024)}, f32[2359296]{0:T(1024)}) async-done(((f32[1769472]{0:T(1024)}, f32[589824]{0:T(1024)}, f32[2359296]{0:T(1024)}, f32[2359296]{0:T(1024)}), (f32[1769472]{0:T(1024)}, f32[589824]{0:T(1024)}, f32[2359296]{0:T(1024)}, f32[2359296]{0:T(1024)})) %all-reduce.31.cloned.1.call-update) | async-done | bytes 28311568
  (377 shorter events, 246.3 us)
Async XLA Ops:
  7.2 49.3 %all-gather.12.cloned.1.call-start = ((), (), s32[]{:S(2)}) async-start(), calls=%async_computation.1 | async-start | bytes 1253376 | tf_op jit(solution)/shard_map/all_gather | solution.py:317
  7.9 92.1 %all-gather.10.cloned.1.call-start = ((), (), s32[]{:S(2)}) async-start(), calls=%async_computation | async-start | bytes 3760128 | tf_op jit(solution)/shard_map/all_gather | solution.py:316
  8.7 146.1 %all-gather.14.cloned.1.call-start = ((), (), s32[]{:S(2)}) async-start(), calls=%async_computation.2 | async-start | bytes 5013504 | tf_op jit(solution)/shard_map/all_gather | solution.py:319
  9.4 199.4 %all-gather.16.cloned.1.call-start = ((), (), s32[]{:S(2)}) async-start(), calls=%async_computation.3 | async-start | bytes 5013504 | tf_op jit(solution)/shard_map/all_gather | solution.py:320
  10.0 314.3 %all-gather.18.cloned.1.call-start = ((), (), s32[]{:S(2)}) async-start(), calls=%async_computation.4 | async-start | bytes 1216512 | tf_op jit(solution)/shard_map/all_gather | solution.py:327
  10.6 313.7 %all-gather.22.cloned.1.call-start = ((), (), s32[]{:S(2)}) async-start(), calls=%async_computation.6 | async-start | bytes 1216512 | tf_op jit(solution)/shard_map/all_gather | solution.py:329
  11.1 368.2 %all-gather.20.cloned.1.call-start = ((), (), s32[]{:S(2)}) async-start(), calls=%async_computation.5 | async-start | bytes 2433024 | tf_op jit(solution)/shard_map/all_gather | solution.py:328
  11.9 432.8 %all-gather.24.cloned.1.call-start = ((), (), s32[]{:S(2)}) async-start(), calls=%async_computation.7 | async-start | bytes 4866048 | tf_op jit(solution)/shard_map/all_gather | solution.py:330
  12.6 497.3 %all-gather.26.cloned.1.call-start = ((), (), s32[]{:S(2)}) async-start(), calls=%async_computation.8 | async-start | bytes 4866048 | tf_op jit(solution)/shard_map/all_gather | solution.py:331
  13.4 1135.9 %all-reduce.29.cloned.1.call-start = ((), (), s32[]{:S(2)}) async-start(), calls=%async_computation.9 | async-start | bytes 56623104
  53.9 154.9 %copy-start.54 = (s32[192]{0:T(256)}, s32[192]{0:T(256)S(1)}, u32[]{:S(2)}) copy-start(s32[192]{0:T(256)S(1)} %select_reduce_fusion) | copy-start | bytes 2308
  54.8 154.1 %copy-start.30 = (pred[3,64,64]{1,2,0:T(32,128)(4,1)}, pred[3,64,64]{1,2,0:T(32,128)(4,1)S(1)}, u32[]{:S(2)}) copy-start(pred[3,64,64]{1,2,0:T(32,128)(4,1)S(1)} %broadcast_and_fusion) | copy-start | bytes 36868
  241.2 42.4 %copy-start.53 = (f32[12,192]{1,0:T(8,128)}, f32[12,192]{1,0:T(8,128)S(1)}, u32[]{:S(2)}) copy-start(f32[12,192]{1,0:T(8,128)S(1)} %get-tuple-element.704) | copy-start | bytes 27652
  241.3 42.4 %copy-start.63 = (bf16[24]{0:T(256)(128)(2,1)S(1)}, bf16[24]{0:T(256)(128)(2,1)}, u32[]{:S(2)}) copy-start(bf16[24]{0:T(256)(128)(2,1)} %param.46) | copy-start | bytes 148
  241.3 42.6 %copy-start.64 = (bf16[24]{0:T(256)(128)(2,1)S(1)}, bf16[24]{0:T(256)(128)(2,1)}, u32[]{:S(2)}) copy-start(bf16[24]{0:T(256)(128)(2,1)} %param.47) | copy-start | bytes 148
  241.3 42.9 %copy-start.65 = (bf16[24]{0:T(256)(128)(2,1)S(1)}, bf16[24]{0:T(256)(128)(2,1)}, u32[]{:S(2)}) copy-start(bf16[24]{0:T(256)(128)(2,1)} %param.48) | copy-start | bytes 148
  241.3 82.9 %copy-start.41 = (bf16[1,192,768]{2,1,0:T(8,128)(2,1)S(1)}, bf16[1,192,768]{2,1,0:T(8,128)(2,1)}, u32[]{:S(2)}) copy-start(bf16[1,192,768]{2,1,0:T(8,128)(2,1)} %param.37) | copy-start | bytes 884740
  244.4 265.6 %collective-permute-start = (bf16[192,768]{1,0:T(8,128)(2,1)S(1)}, bf16[192,768]{1,0:T(8,128)(2,1)S(1)}, u32[]{:S(2)}, u32[]{:S(2)}) collective-permute-start(bf16[192,768]{1,0:T(8,128)(2,1)S(1)} %convert_element_type.279), channel_id=1, source_target_pairs={{0,16},{1,17},{2,18},{3,19},{4,20},{5,21},{6,22},{7,23},{8,24},{9,... | collective-permute-start | bytes 884744 | tf_op jit(solution)/shard_map/ppermute | solution.py:17
  564.1 1077.0 %all-reduce.31.cloned.1.call-start = ((), (), s32[]{:S(2)}) async-start(), calls=%async_computation.10 | async-start | bytes 56623104
  564.2 168.0 %copy-start.4 = (bf16[1,768,768]{2,1,0:T(8,128)(2,1)S(1)}, bf16[1,768,768]{2,1,0:T(8,128)(2,1)}, u32[]{:S(2)}) copy-start(bf16[1,768,768]{2,1,0:T(8,128)(2,1)} %all-gather.12.cloned.1.call-done) | copy-start | bytes 3538948
  565.4 164.9 %collective-permute-start.1 = (bf16[192,768]{1,0:T(8,128)(2,1)S(1)}, bf16[192,768]{1,0:T(8,128)(2,1)S(1)}, u32[]{:S(2)}, u32[]{:S(2)}) collective-permute-start(bf16[192,768]{1,0:T(8,128)(2,1)S(1)} %convert_element_type.285), channel_id=1, source_target_pairs={{16,0},{17,1},{18,2},{19,3},{20,4},{21,5},{22,6},{23,7},{24,8},{25... | collective-permute-start | bytes 884744 | tf_op jit(solution)/shard_map/ppermute | solution.py:17
  892.7 77.9 %copy-start.9 = (f32[192,768]{1,0:T(8,128)S(1)}, f32[192,768]{1,0:T(8,128)}, u32[]{:S(2)}) copy-start(f32[192,768]{1,0:T(8,128)} %get-tuple-element.720) | copy-start | bytes 1769476
  892.7 77.9 %copy-start.12 = (f32[192,768]{1,0:T(8,128)S(1)}, f32[192,768]{1,0:T(8,128)}, u32[]{:S(2)}) copy-start(f32[192,768]{1,0:T(8,128)} %get-tuple-element.718) | copy-start | bytes 1769476
  892.7 77.9 %copy-start.34 = (f32[192,768]{1,0:T(8,128)S(1)}, f32[192,768]{1,0:T(8,128)}, u32[]{:S(2)}) copy-start(f32[192,768]{1,0:T(8,128)} %copy-done.33) | copy-start | bytes 1769476
  (27 other events, 165.3 us)
Sparse Core Ops, SparseCore 0:
  10.3 41.1 all-gather.11
  53.8 46.1 all-gather.9
  102.3 52.3 all-gather.13
  156.9 51.9 all-gather.15
  211.6 52.8 all-gather.17
  267.2 53.0 all-gather.21
  323.2 56.1 all-gather.19
  382.3 62.3 all-gather.23
  447.6 62.3 all-gather.25
  564.3 584.9 all-reduce.28
  1154.1 487.0 all-reduce.30
where the time goes:
time: 1680 us; the launch traced here: 1660 us
  waiting for transfers between devices  1130 us (67%)
  blocking collectives  174 us (10%)
  local copies, waits for them, and re-layouts  146 us (9%)
  matrix products  114 us (7%)
  starting transfers between devices  41 us (2%)
  other arithmetic  28.9 us (2%)
  between operations  18.7 us (1%)
    unnamed x13, waiting for transfers between devices  629 us
    ppermute x2, waiting for transfers between devices, from_behind(): return lax.ppermute(block, axis, route)  161 us
    unnamed x3, blocking collectives  138 us
    all_gather x1, waiting for transfers between devices, shards(): lax.all_gather(cross_up, ('tower', 'dp'), axis=0, tiled=True)  65.3 us
    all_gather x1, waiting for transfers between devices, shards(): lax.all_gather(cross_down, ('tower', 'dp'), axis=0, tiled=True)  65.3 us
    all_gather x1, waiting for transfers between devices, shards(): lax.all_gather(cross_keyval, ('tower', 'dp'), axis=0, tiled=True)  55.1 us
    all_gather x1, waiting for transfers between devices, shards(): lax.all_gather(mlp_up, 'dp', axis=1, tiled=True)  54.7 us
    all_gather x1, waiting for transfers between devices, shards(): lax.all_gather(mlp_down, 'dp', axis=1, tiled=True)  54.1 us
  transfers between devices with their start and end apart: 13, of which 9 were waited for; matrix products, arithmetic and copies ran while one was open for 14% of the time, Pallas kernels for 0%

commit v1 on v0

v1 whole, which is shorter than its diff:
```python
import functools

import jax
import jax.numpy as jnp
from jax import lax
from jax.experimental import pallas as pl
from jax.experimental.pallas import tpu as pltpu
from jax.sharding import PartitionSpec as P

HD = 64
CAP_LEN = 64
EPSILON = 1e-06
NEGATIVE = -1000000000.0

MESH_ID = pl.DeviceIdType.MESH
ANY = pl.BlockSpec(memory_space=pl.ANY)
VMEM = pl.BlockSpec(memory_space=pltpu.VMEM)


class Net:
    def __init__(self, lines):
        self.lines = lines
        self.tower = lax.axis_index("tower")
        self.dp = lax.axis_index("dp")
        self.core = self.dp % 2
        self.y = (self.dp // 2) % 2
        self.z = self.dp // 4
        self.chip = self.dp // 2
        self.text = self.tower == 1
        self.image = self.tower == 0
        self.low = self.z > 0
        self.high = self.z < lines - 1
        self.sends = []

    def target(self, way):
        if way == "core":
            return (self.tower, self.dp + 1 - 2 * self.core)
        if way == "y":
            return (self.tower, self.dp + 2 - 4 * self.y)
        if way == "x":
            return (1 - self.tower, self.dp)
        if way == "up":
            return (self.tower, jnp.minimum(self.dp + 4, 4 * self.lines - 1))
        return (self.tower, jnp.maximum(self.dp - 4, 0))

    def beyond(self, k):
        return (self.tower, 4 * lax.rem(self.z + k, self.lines) + self.dp % 4)

    def barrier(self):
        sem = pltpu.get_barrier_semaphore()
        partners = [self.target(way) for way in ("core", "y", "x")]
        partners += [self.beyond(k) for k in range(1, self.lines)]
        for partner in partners:
            pl.semaphore_signal(sem, inc=1, device_id=partner, device_id_type=MESH_ID)
        pl.semaphore_wait(sem, len(partners))

    def copy(self, way, src, dst, send_sem, recv_sem):
        return pltpu.make_async_remote_copy(
            src_ref=src,
            dst_ref=dst,
            send_sem=send_sem,
            recv_sem=recv_sem,
            device_id=self.target(way),
            device_id_type=MESH_ID,
        )

    def send(self, way, src, dst, send_sem, recv_sem, there=None):
        copy = self.copy(way, src, dst, send_sem, recv_sem)
        when(there, copy.start)
        self.sends.append((copy, there))

    def arrive(self, src, send_sem, recv_sem, there=None):
        copy = self.copy("core", src, src, send_sem, recv_sem)
        when(there, copy.wait_recv)

    def finish(self):
        for copy, there in self.sends:
            when(there, copy.wait_send)
        self.sends = []


def when(there, act):
    if there is None:
        act()
    else:
        pl.when(there)(act)


def both(*conditions):
    kept = [c for c in conditions if c is not None]
    if not kept:
        return None
    result = kept[0]
    for c in kept[1:]:
        result = jnp.logical_and(result, c)
    return result


class Gather:
    def __init__(self, net, own, place, crossing, send_sem, recv_sem, local_sem, everywhere=False):
        self.net, self.own, self.place, self.crossing = net, own, place, crossing
        self.send_sem, self.recv_sem, self.local_sem = send_sem, recv_sem, local_sem
        lines = net.lines
        self.at_z, self.at_y, self.at_x, self.at_core = 0, 2 * lines, 3 * lines, 5 * lines
        self.to_x = net.image if crossing else None
        self.to_core = net.text if crossing and not everywhere else None

    @staticmethod
    def sems(lines):
        return 9 * lines

    def piece(self, chip, tower=None, core=None):
        net = self.net
        return self.place(
            net.tower if tower is None else tower, chip, net.core if core is None else core
        )

    def pass_on(self, chip, src, there=None, tower=None):
        net = self.net
        dst = self.piece(chip, tower)
        plane = net.tower if tower is None else tower
        if self.crossing and tower is None:
            s = self.at_x + chip
            net.send("x", src, dst, self.send_sem.at[s], self.recv_sem.at[s], both(there, net.image))
        s = self.at_core + plane * 2 * net.lines + chip
        net.send("core", src, dst, self.send_sem.at[s], self.recv_sem.at[s], both(there, self.to_core))

    def start(self):
        net = self.net
        dst = self.piece(net.chip)
        self.local = pltpu.make_async_copy(self.own, dst, self.local_sem)
        self.local.start()
        for way, there, slot in (("up", net.high, 1), ("down", net.low, net.lines + 1)):
            s = self.at_z + slot
            net.send(way, self.own, dst, self.send_sem.at[s], self.recv_sem.at[s], there)
        s = self.at_y + net.z
        net.send("y", self.own, dst, self.send_sem.at[s], self.recv_sem.at[s])
        self.pass_on(net.chip, self.own)

    def hop(self, k):
        net = self.net
        for way, there, further, sign, base in (
            ("up", net.z >= k, net.high, -1, 0),
            ("down", net.z + k < net.lines, net.low, 1, net.lines),
        ):
            z = jnp.clip(net.z + sign * k, 0, net.lines - 1)
            chip = 2 * z + net.y
            src = self.piece(chip)
            s = self.at_z + base + k
            net.arrive(src, self.send_sem.at[s], self.recv_sem.at[s], there)
            if k + 1 < net.lines:
                s = s + 1
                net.send(way, src, src, self.send_sem.at[s], self.recv_sem.at[s], both(there, further))
            s = self.at_y + z
            net.send("y", src, src, self.send_sem.at[s], self.recv_sem.at[s], there)
            self.pass_on(chip, src, there)

    def beside(self, k):
        net = self.net
        ways = ((None, 0),) if k == 0 else ((net.z >= k, -k), (net.z + k < net.lines, k))
        for there, offset in ways:
            z = jnp.clip(net.z + offset, 0, net.lines - 1)
            chip = 2 * z + 1 - net.y
            src = self.piece(chip)
            s = self.at_y + z
            net.arrive(src, self.send_sem.at[s], self.recv_sem.at[s], there)
            self.pass_on(chip, src, there)

    def from_image(self, k):
        if not self.crossing:
            return
        net = self.net
        ways = ((None, 0),) if k == 0 else ((net.z >= k, -k), (net.z + k < net.lines, k))
        for there, offset in ways:
            z = jnp.clip(net.z + offset, 0, net.lines - 1)
            for y in (net.y, 1 - net.y):
                chip = 2 * z + y
                src = self.piece(chip, 0)
                s = self.at_x + chip
                net.arrive(src, self.send_sem.at[s], self.recv_sem.at[s], both(there, net.text))
                self.pass_on(chip, src, both(there, net.text), 0)

    def done(self):
        net = self.net
        self.local.wait()

        def all_of(tower, base):
            def one(chip, carry):
                s = self.at_core + base + chip
                src = self.piece(chip, tower, 1 - net.core)
                net.arrive(src, self.send_sem.at[s], self.recv_sem.at[s])
                return carry

            def run():
                lax.fori_loop(0, 2 * net.lines, one, 0)

            return run

        when(self.to_core, all_of(net.tower, net.tower * 2 * net.lines))
        if self.crossing:
            when(net.text, all_of(0, 0))


def gather_kernel(
    lines, wide, half, own_a, own_d, pack, own_cd, own_g, full_a, full_d, full_ca, full_cd, full_g,
    swap, block, send_sem, recv_sem, local_sem, swap_sem,
):
    net = Net(lines)
    net.barrier()
    rows, depth = own_a.shape[0], own_d.shape[0]
    few, part = pack.shape[1], own_cd.shape[0]
    swapped = net.copy("core", pack.at[1 - net.core], swap, swap_sem.at[0], swap_sem.at[1])
    swapped.start()

    def columns(first, last):
        return lambda tower, chip, core: full_a.at[
            pl.ds(pl.multiple_of((2 * chip + core) * rows, rows), rows), first:last
        ]

    def plan(index, own, place, crossing, everywhere=False):
        return Gather(
            net, own, place, crossing, send_sem.at[index], recv_sem.at[index], local_sem.at[index], everywhere
        )

    jobs = [
        plan(0, own_g, lambda tower, chip, core: full_g.at[tower, 2 * chip + core], True, True),
        plan(1, own_a.at[:, 0:wide], columns(0, wide), False),
        plan(2, own_a.at[:, wide:], columns(wide, own_a.shape[1]), False),
        plan(
            3,
            own_d,
            lambda tower, chip, core: full_d.at[
                pl.ds(pl.multiple_of((2 * chip + core) * depth, depth), depth), :
            ],
            False,
        ),
        plan(
            4,
            block,
            lambda tower, chip, core: full_ca.at[
                core, pl.ds(pl.multiple_of((tower * 2 * lines + chip) * 2 * few, 2 * few), 2 * few), :
            ],
            True,
        ),
        plan(
            5,
            own_cd,
            lambda tower, chip, core: full_cd.at[
                pl.ds(
                    pl.multiple_of((tower * 4 * lines + 2 * chip + core) * part, part), part
                ),
                :,
            ],
            True,
        ),
    ]
    for job in jobs[:4]:
        job.start()
    swapped.wait()
    first = net.core == 0
    mine = pack[net.core]
    theirs = swap[...]
    block[0:few] = jnp.where(first, mine, theirs).astype(jnp.bfloat16)
    block[few:] = jnp.where(first, theirs, mine).astype(jnp.bfloat16)
    for job in jobs[4:]:
        job.start()
    for job in jobs:
        job.beside(0)
        job.from_image(0)
    for k in range(1, lines):
        for job in jobs:
            job.hop(k)
        for job in jobs:
            job.beside(k)
            job.from_image(k)
    for job in jobs:
        job.done()
    net.finish()


def gather(lines, wide, own_a, own_d, pack, own_cd, own_g):
    count = 4 * lines
    half, few, width = pack.shape
    jobs = 6
    return pl.pallas_call(
        functools.partial(gather_kernel, lines, wide, width),
        out_shape=(
            jax.ShapeDtypeStruct((count * own_a.shape[0], own_a.shape[1]), jnp.bfloat16),
            jax.ShapeDtypeStruct((count * own_d.shape[0], own_d.shape[1]), jnp.bfloat16),
            jax.ShapeDtypeStruct((2, 2 * count * few, width), jnp.bfloat16),
            jax.ShapeDtypeStruct((2 * count * own_cd.shape[0], own_cd.shape[1]), jnp.bfloat16),
            jax.ShapeDtypeStruct((2, count) + own_g.shape, jnp.float32),
        ),
        in_specs=[ANY, ANY, VMEM, ANY, ANY],
        out_specs=[ANY] * 5,
        scratch_shapes=[
            pltpu.VMEM((few, width), jnp.float32),
            pltpu.VMEM((2 * few, width), jnp.bfloat16),
            pltpu.SemaphoreType.DMA((jobs, Gather.sems(lines))),
            pltpu.SemaphoreType.DMA((jobs, Gather.sems(lines))),
            pltpu.SemaphoreType.DMA((jobs,)),
            pltpu.SemaphoreType.DMA((2,)),
        ],
        compiler_params=pltpu.CompilerParams(
            collective_id=0, has_side_effects=True, vmem_limit_bytes=32 << 20
        ),
    )(own_a, own_d, pack, own_cd, own_g)


class Scatter:
    def __init__(self, net, crossing, grad, own, beside, near, far, sems):
        self.net, self.crossing, self.grad = net, crossing, grad
        self.own, self.rcv, self.near, self.far = own, beside, near, far
        self.send_sem, self.recv_sem, self.local_sem = sems

    def add(self, pairs, out):
        shape = out.shape
        step = 16

        def one(i, carry):
            rows = pl.ds(pl.multiple_of(i * step, step), step)
            total = pairs[0][rows, :].astype(jnp.float32)
            for other in pairs[1:]:
                total = total + other[rows, :].astype(jnp.float32)
            out[rows, :] = total.astype(out.dtype)
            return carry

        lax.fori_loop(0, shape[0] // step, one, 0)

    @staticmethod
    def sems(lines):
        return 1 + 5 * lines

    def plane(self):
        return self.own.at[self.net.tower] if self.crossing else self.own

    def start(self):
        net = self.net
        there = net.text if self.crossing else None
        self.load = pltpu.make_async_copy(self.grad(net.core), self.own, self.local_sem)
        when(there, self.load.start)
        net.send(
            "core", self.grad(1 - net.core), self.rcv, self.send_sem.at[0], self.recv_sem.at[0], there
        )

    def chips(self, k):
        net = self.net
        if k == 0:
            return ((None, net.z),)
        return (
            (net.z + k < net.lines, jnp.minimum(net.z + k, net.lines - 1)),
            (net.z >= k, jnp.maximum(net.z - k, 0)),
        )

    def cores(self):
        net = self.net
        lines = net.lines
        there = net.text if self.crossing else None

        def arrived():
            self.load.wait()

        when(there, arrived)
        net.arrive(self.rcv, self.send_sem.at[0], self.recv_sem.at[0], there)

        def sum_of(own, rcv):
            def one(i, carry):
                self.add([own.at[i], rcv.at[i]], own.at[i])
                return carry

            lax.fori_loop(0, 2 * lines, one, 0)

        if self.crossing:

            def text():
                sum_of(self.own.at[0], self.rcv.at[0])

            when(there, text)
            for k in range(lines - 1, -1, -1):
                for there_k, z in self.chips(k):
                    for y in (1 - net.y, net.y):
                        chip = 2 * z + y
                        s = 1 + chip
                        net.send(
                            "x",
                            self.own.at[0, chip],
                            self.own.at[0, chip],
                            self.send_sem.at[s],
                            self.recv_sem.at[s],
                            both(there_k, net.text),
                        )

            def text_too():
                sum_of(self.own.at[1], self.rcv.at[1])

            when(there, text_too)
        else:
            sum_of(self.own, self.rcv)

    def across(self):
        net = self.net
        lines = net.lines
        for k in range(lines - 1, -1, -1):
            for there, z in self.chips(k):
                chip = 2 * z + 1 - net.y
                if self.crossing:
                    s = 1 + chip
                    net.arrive(
                        self.own.at[0, chip],
                        self.send_sem.at[s],
                        self.recv_sem.at[s],
                        both(there, net.image),
                    )
                s = 1 + 2 * lines + z
                net.send(
                    "y", self.plane().at[chip], self.near.at[z], self.send_sem.at[s], self.recv_sem.at[s], there
                )

    def along(self):
        net = self.net
        lines = net.lines
        own = self.plane()
        for k in range(lines - 1, 0, -1):
            for way, (there, z) in zip(("up", "down"), self.chips(k)):
                chip = 2 * z + net.y
                up = way == "up"
                base = 1 + 3 * lines if up else 1 + 4 * lines
                if self.crossing:
                    s = 1 + chip
                    net.arrive(
                        self.own.at[0, chip],
                        self.send_sem.at[s],
                        self.recv_sem.at[s],
                        both(there, net.image),
                    )
                s = 1 + 2 * lines + z
                net.arrive(self.near.at[z], self.send_sem.at[s], self.recv_sem.at[s], there)
                more = net.low if up else net.high
                s = base + z
                net.arrive(self.far.at[z], self.send_sem.at[s], self.recv_sem.at[s], both(there, more))

                def with_far():
                    self.add([own.at[chip], self.near.at[z], self.far.at[z]], own.at[chip])

                def without():
                    self.add([own.at[chip], self.near.at[z]], own.at[chip])

                when(both(there, more), with_far)
                when(both(there, jnp.logical_not(more)), without)
                slot = z
                if up:
                    target = self.far.at[slot]
                else:
                    last = jnp.where(z == net.z - 1, lines, z)
                    target = self.far.at[last]
                net.send(way, own.at[chip], target, self.send_sem.at[s], self.recv_sem.at[s], there)

    def total(self, out):
        net = self.net
        lines = net.lines
        own = self.plane()
        chip = net.chip
        if self.crossing:
            s = 1 + chip
            net.arrive(
                self.own.at[0, chip], self.send_sem.at[s], self.recv_sem.at[s], net.image
            )
        s = 1 + 2 * lines + net.z
        net.arrive(self.near.at[net.z], self.send_sem.at[s], self.recv_sem.at[s])
        s = 1 + 3 * lines + net.z
        net.arrive(self.far.at[net.z], self.send_sem.at[s], self.recv_sem.at[s], net.low)
        s = 1 + 4 * lines + net.z
        net.arrive(self.far.at[lines], self.send_sem.at[s], self.recv_sem.at[s], net.high)
        here = [own.at[chip], self.near.at[net.z]]
        from_low, from_high = self.far.at[net.z], self.far.at[lines]
        when(both(net.low, net.high), lambda: self.add(here + [from_low, from_high], out))
        when(jnp.logical_not(net.low), lambda: self.add(here + [from_high], out))
        when(jnp.logical_not(net.high), lambda: self.add(here + [from_low], out))


class Small:
    def __init__(self, net, mine, arrived, sums, wide, send_sem, recv_sem):
        self.net, self.mine, self.arrived, self.sums, self.wide = net, mine, arrived, sums, wide
        self.send_sem, self.recv_sem = send_sem, recv_sem

    def exchange(self, step):
        src = self.mine if step == 0 else self.sums.at[step - 1]
        self.net.send(
            ("core", "y", "x")[step],
            src,
            self.arrived.at[step],
            self.send_sem.at[step],
            self.recv_sem.at[step],
        )

    def collect(self, step):
        self.net.arrive(self.arrived.at[step], self.send_sem.at[step], self.recv_sem.at[step])
        src = self.mine if step == 0 else self.sums.at[step - 1]
        self.sums[step] = src[...] + self.arrived[step]

    def spread(self):
        net = self.net
        for k in range(1, net.lines):
            s = 2 + k
            copy = pltpu.make_async_remote_copy(
                src_ref=self.sums.at[2],
                dst_ref=self.wide.at[k - 1],
                send_sem=self.send_sem.at[s],
                recv_sem=self.recv_sem.at[s],
                device_id=net.beyond(k),
                device_id_type=MESH_ID,
            )
            copy.start()
            net.sends.append((copy, None))

    def total(self, out):
        total = self.sums[2]
        for k in range(1, self.net.lines):
            s = 2 + k
            self.net.arrive(self.wide.at[k - 1], self.send_sem.at[s], self.recv_sem.at[s])
            total = total + self.wide[k - 1]
        out[...] = total


def scatter_kernel(
    lines, wide, cuts, g_a, g_d, g_ca, g_cd, vec,
    o_qkv, o_out, o_up, o_d, o_cq, o_ckv, o_co, o_cu, o_cd, o_vec,
    *scratch,
):
    net = Net(lines)
    net.barrier()
    buffers = [scratch[4 * i : 4 * i + 4] for i in range(5)]
    send_sem, recv_sem, local_sem, fin, swap, swap_sem, arrived, sums, spread, s_send, s_recv = scratch[20:]
    small = Small(net, vec, arrived, sums, spread, s_send, s_recv)
    width = g_ca.shape[-1]
    few = g_ca.shape[-2]

    def job(index, crossing, grad):
        return Scatter(
            net,
            crossing,
            grad,
            *buffers[index],
            (send_sem.at[index], recv_sem.at[index], local_sem.at[index]),
        )

    s_d = job(0, False, lambda core: g_d.at[:, core])
    c_d = job(1, True, lambda core: g_cd.at[:, :, core])
    s_up = job(2, False, lambda core: g_a.at[:, core, :, pl.ds(wide, g_a.shape[-1] - wide)])
    c_a = job(3, True, lambda core: g_ca.at[core])
    s_qkv = job(4, False, lambda core: g_a.at[:, core, :, pl.ds(0, wide)])

    small.exchange(0)
    s_d.start()
    c_d.start()
    s_d.cores()
    s_d.across()
    s_up.start()
    small.collect(0)
    small.exchange(1)
    c_d.cores()
    c_a.start()
    s_d.along()
    s_up.cores()
    s_qkv.start()
    c_d.across()
    s_up.across()
    small.collect(1)
    small.exchange(2)
    c_a.cores()
    c_d.along()
    s_qkv.cores()
    s_d.total(o_d)
    c_a.across()
    s_qkv.across()
    small.collect(2)
    small.spread()
    s_up.along()
    c_d.total(o_cd)
    c_a.along()
    s_up.total(fin.at[0:few, 0 : g_a.shape[-1] - wide])
    o_out[...] = fin[0:few, 0 : o_out.shape[1]]
    o_up[...] = fin[0:few, o_out.shape[1] : g_a.shape[-1] - wide]
    s_qkv.along()
    c_a.total(fin.at[0:few, 0:width])
    share = few // 2
    other = 1 - net.core
    swapped = net.copy(
        "core",
        fin.at[pl.ds(pl.multiple_of(other * share, share), share), 0:width],
        swap,
        swap_sem.at[0],
        swap_sem.at[1],
    )
    swapped.start()
    s_qkv.total(o_qkv)
    small.total(o_vec)
    swapped.wait()
    mine = fin[pl.ds(pl.multiple_of(net.core * share, share), share), 0:width]
    theirs = swap[...]
    first = net.core == 0
    left = jnp.where(first, mine, theirs)
    right = jnp.where(first, theirs, mine)
    at = 0
    for out, n in zip((o_cq, o_ckv, o_co, o_cu), cuts):
        out[:, 0:n] = left[:, at : at + n]
        out[:, n:] = right[:, at : at + n]
        at += n
    net.finish()


def scatter(lines, g_a, g_d, g_ca, g_cd, vec, parts, cuts):
    chips = 2 * lines
    wide = parts[0]
    rows = g_a.shape[2]
    few = g_ca.shape[3]
    bf16, f32 = jnp.bfloat16, jnp.float32

    def buffers(crossing, rows, n):
        whole = ((2, chips, rows, n) if crossing else (chips, rows, n))
        return [
            pltpu.VMEM(whole, bf16),
            pltpu.VMEM(whole, bf16),
            pltpu.VMEM((lines, rows, n), bf16),
            pltpu.VMEM((lines + 1, rows, n), bf16),
        ]

    scratch = (
        buffers(False, g_d.shape[2], g_d.shape[3])
        + buffers(True, g_cd.shape[3], g_cd.shape[4])
        + buffers(False, rows, g_a.shape[3] - wide)
        + buffers(True, few, g_ca.shape[4])
        + buffers(False, rows, wide)
        + [
            pltpu.SemaphoreType.DMA((5, Scatter.sems(lines))),
            pltpu.SemaphoreType.DMA((5, Scatter.sems(lines))),
            pltpu.SemaphoreType.DMA((5,)),
            pltpu.VMEM((rows, max(g_a.shape[3] - wide, g_ca.shape[4])), f32),
            pltpu.VMEM((few // 2, g_ca.shape[4]), f32),
            pltpu.SemaphoreType.DMA((2,)),
            pltpu.VMEM((3,) + vec.shape, f32),
            pltpu.VMEM((3,) + vec.shape, f32),
            pltpu.VMEM((lines - 1,) + vec.shape, f32),
            pltpu.SemaphoreType.DMA((2 + lines,)),
            pltpu.SemaphoreType.DMA((2 + lines,)),
        ]
    )
    share = few // 2
    outs = [
        (rows, parts[0]),
        (rows, parts[1]),
        (rows, parts[2]),
        (g_d.shape[2], g_d.shape[3]),
        (share, 2 * cuts[0]),
        (share, 2 * cuts[1]),
        (share, 2 * cuts[2]),
        (share, 2 * cuts[3]),
        (g_cd.shape[3], g_cd.shape[4]),
        vec.shape,
    ]
    return pl.pallas_call(
        functools.partial(scatter_kernel, lines, wide, cuts),
        out_shape=tuple(jax.ShapeDtypeStruct(s, f32) for s in outs),
        in_specs=[ANY, ANY, ANY, ANY, VMEM],
        out_specs=[VMEM] * len(outs),
        scratch_shapes=scratch,
        compiler_params=pltpu.CompilerParams(
            collective_id=1, has_side_effects=True, vmem_limit_bytes=62 << 20
        ),
    )(g_a, g_d, g_ca, g_cd, vec)


def plain_gather(own_a, own_d, pack, own_cd, own_g):
    axes = ("tower", "dp")
    tiles = lax.all_gather(own_g, axes, axis=0)
    return (
        lax.all_gather(own_a, "dp", axis=0, tiled=True),
        lax.all_gather(own_d, "dp", axis=0, tiled=True),
        lax.all_gather(pack.astype(jnp.bfloat16), axes, axis=1, tiled=True),
        lax.all_gather(own_cd, axes, axis=0, tiled=True),
        tiles.reshape((2, -1) + own_g.shape),
    )


def plain_scatter(g_a, g_d, g_ca, g_cd, vec, parts, cuts):
    axes = ("tower", "dp")

    def added(grad, over, axis):
        return lax.psum_scatter(
            grad.astype(jnp.float32), over, scatter_dimension=axis, tiled=True
        )

    a = added(g_a.reshape(-1, g_a.shape[-1]), "dp", 0)
    d = added(g_d.reshape(-1, g_d.shape[-1]), "dp", 0)
    ca = added(g_ca.reshape(2, -1, g_ca.shape[-1]), axes, 1)
    cd = added(g_cd.reshape(-1, g_cd.shape[-1]), axes, 0)
    at = [sum(cuts[:i]) for i in range(len(cuts) + 1)]
    cross = [
        jnp.concatenate([ca[0][:, i:j], ca[1][:, i:j]], axis=1) for i, j in zip(at[:-1], at[1:])
    ]
    first, second = parts[0], parts[0] + parts[1]
    self_parts = [a[:, :first], a[:, first:second], a[:, second:]]
    return (*self_parts, d, *cross, cd, lax.psum(vec, axes))


def layer_norm(value_matrix, norm_gain):
    center = value_matrix - jnp.mean(value_matrix, axis=-1, keepdims=True)
    spread = jnp.mean(center * center, axis=-1, keepdims=True)
    return center * lax.rsqrt(spread + EPSILON) * norm_gain


def norm_back(value_matrix, norm_gain, grad_out):
    result, puller = jax.vjp(layer_norm, value_matrix, norm_gain)
    return puller(grad_out)


def dot(a, b):
    return jnp.dot(a, b, preferred_element_type=jnp.float32)


def dot_tn(a, b):
    return jnp.einsum("rd,re->de", a, b, preferred_element_type=jnp.float32)


def dot_nt(a, b):
    return jnp.einsum("re,de->rd", a, b, preferred_element_type=jnp.float32)


def low(value_matrix):
    return value_matrix.astype(jnp.bfloat16)


def masks(counts, lengths, row_count, decoder):
    row_index = jnp.arange(row_count, dtype=jnp.int32)
    bounds = jnp.cumsum(counts)
    image_of = jnp.sum((row_index[:, None] >= bounds[None, :]).astype(jnp.int32), axis=1)
    caption_of = row_index // CAP_LEN
    in_place = row_index - caption_of * CAP_LEN
    caption_slots = jnp.arange(lengths.shape[0], dtype=jnp.int32)
    length_rows = jnp.sum(
        jnp.where(caption_of[:, None] == caption_slots[None, :], lengths[None, :], 0), axis=1
    )
    valid_rows = in_place < length_rows
    image_mask = image_of[:, None] == image_of[None, :]
    text_mask = (
        (caption_of[:, None] == caption_of[None, :])
        & (in_place[None, :] <= in_place[:, None])
        & valid_rows[None, :]
    )
    cross_mask = caption_of[:, None] == image_of[None, :]
    return jnp.where(decoder, text_mask, image_mask), cross_mask, valid_rows


def heads(value_matrix):
    return value_matrix.reshape(value_matrix.shape[0], -1, HD)


def attend(query, key, value, allowed):
    scores = jnp.einsum(
        "qhd,khd->hqk", heads(query), heads(key), preferred_element_type=jnp.float32
    ) * HD ** (-0.5)
    weight = jax.nn.softmax(jnp.where(allowed[None], scores, NEGATIVE), axis=-1)
    mixed = jnp.einsum("hqk,khd->qhd", low(weight), heads(value), preferred_element_type=jnp.float32)
    return low(mixed.reshape(query.shape)), weight


def attend_back(query, key, value, weight, grad_mixed):
    grad_mixed = heads(grad_mixed)
    grad_value = jnp.einsum("hqk,qhd->khd", low(weight), grad_mixed, preferred_element_type=jnp.float32)
    grad_weight = jnp.einsum("qhd,khd->hqk", grad_mixed, heads(value), preferred_element_type=jnp.float32)
    grad_score = low(
        weight * (grad_weight - jnp.sum(grad_weight * weight, axis=-1, keepdims=True))
    )
    grad_query = jnp.einsum(
        "hqk,khd->qhd", grad_score, heads(key), preferred_element_type=jnp.float32
    ) * HD ** (-0.5)
    grad_key = jnp.einsum(
        "hqk,qhd->khd", grad_score, heads(query), preferred_element_type=jnp.float32
    ) * HD ** (-0.5)
    return tuple(low(g.reshape(query.shape)) for g in (grad_query, grad_key, grad_value))


def mlp_forward(stream, gain, up, down):
    hidden = low(layer_norm(stream, gain))
    wide = dot(hidden, up)
    active = low(jax.nn.gelu(wide))
    return dot(active, down), (hidden, wide, active)


def mlp_back(stream, gain, up, down, stored, grad):
    hidden, wide, active = stored
    branch = low(grad)
    grad_down = dot_tn(active, branch)
    result, puller = jax.vjp(jax.nn.gelu, wide)
    grad_wide = low(puller(dot_nt(branch, down))[0])
    grad_up = dot_tn(hidden, grad_wide)
    grad_stream, grad_gain = norm_back(stream, gain, dot_nt(grad_wide, up))
    return grad + grad_stream, grad_gain, grad_up, grad_down


def squares(value_matrix, row_weight):
    return jnp.sum(row_weight[:, None] * value_matrix * value_matrix)


def shards(
    tokens, cotangent, kept_counts, caption_lengths, attn_gain, qkv_weight, attn_out, mlp_gain,
    mlp_up, mlp_down, query_gain, image_gain, cross_gain, cross_query, cross_keyval, cross_out,
    cross_up, cross_down,
):
    f32 = jnp.float32
    dp_count = lax.axis_size("dp")
    lines = dp_count // 4
    tower, dp = lax.axis_index("tower"), lax.axis_index("dp")
    decoder = tower == 1
    row_count, width = tokens.shape[1:]
    rows = attn_gain.shape[1]
    few = query_gain.shape[0]

    def tile_row(value):
        return jnp.pad(value.astype(f32), (0, 128 - value.shape[0]))

    gain_tile = jnp.stack(
        [tile_row(attn_gain[0]), tile_row(mlp_gain[0])]
        + [tile_row(g) for g in (query_gain, image_gain, cross_gain)]
        + [jnp.zeros((128,), f32)] * 3
    )
    cross_shards = (cross_query, cross_keyval, cross_out, cross_up)
    cuts = tuple(w.shape[1] // 2 for w in cross_shards)
    pack = jnp.stack(
        [
            jnp.concatenate([w[:, h * n : (h + 1) * n] for w, n in zip(cross_shards, cuts)], axis=1)
            for h in range(2)
        ]
    ).astype(f32)
    self_parts = (qkv_weight.shape[2], attn_out.shape[2], mlp_up.shape[2])
    own_a = jnp.concatenate([qkv_weight[0], attn_out[0], mlp_up[0]], axis=1)
    fills = dp_count % 4 == 0 and dp_count > 4 and rows % 16 == 0 and few % 8 == 0
    fills = fills and cross_down.shape[0] % 16 == 0
    own = (own_a, mlp_down[0], pack, cross_down, gain_tile)
    full = gather(lines, self_parts[0], *own) if fills else plain_gather(*own)
    full_a, full_d, full_ca, full_cd, full_g = full
    qkv = full_a[:, : self_parts[0]]
    out = full_a[:, self_parts[0] : self_parts[0] + self_parts[1]]
    up = full_a[:, self_parts[0] + self_parts[1] :]
    down = full_d
    plane_gains = lax.dynamic_index_in_dim(full_g, tower, 0, keepdims=False)
    gain_1 = plane_gains[:, 0, :rows].reshape(-1)
    gain_2 = plane_gains[:, 1, :rows].reshape(-1)
    gain_q, gain_i, gain_c = (full_g[:, :, 2 + i, :few].reshape(-1) for i in range(3))

    stream = tokens[0].astype(f32)
    upstream = cotangent[0].astype(f32)
    allowed, cross_allowed, valid_rows = masks(kept_counts[0], caption_lengths, row_count, decoder)
    row_weight = jnp.where(decoder, valid_rows, True).astype(f32)

    normed = low(layer_norm(stream, gain_1))
    joined = low(dot(normed, qkv))
    query, key, value = jnp.split(joined, 3, axis=1)
    mixed, weight = attend(query, key, value, allowed)
    attn_branch = dot(mixed, out)
    middle = stream + attn_branch
    mlp_branch, mlp_stored = mlp_forward(middle, gain_2, up, down)
    layer_y = middle + mlp_branch
    image_rows = low(layer_y)
    arrived = lax.ppermute(image_rows, "tower", [(0, 1)])

    def run_cross(operands):
        text_y, image_in = operands
        at = [0]
        for n in cuts:
            at.append(at[-1] + n)
        cq, ckv, co, cu = (
            jnp.concatenate([full_ca[0][:, a:b], full_ca[1][:, a:b]], axis=1)
            for a, b in zip(at[:-1], at[1:])
        )
        image_in = image_in.astype(f32)
        image_normed = low(layer_norm(image_in, gain_i))
        keyval = low(dot(image_normed, ckv))
        c_key, c_value = jnp.split(keyval, 2, axis=1)
        c_normed = low(layer_norm(text_y, gain_q))
        c_query = low(dot(c_normed, cq))
        c_mixed, c_weight = attend(c_query, c_key, c_value, cross_allowed)
        c_branch = dot(c_mixed, co)
        c_middle = text_y + c_branch
        c_mlp, c_stored = mlp_forward(c_middle, gain_c, cu, full_cd)
        final_rows = c_middle + c_mlp
        grad_middle, grad_gain_c, grad_cu, grad_cd = mlp_back(
            c_middle, gain_c, cu, full_cd, c_stored, upstream
        )
        grad_branch = low(grad_middle)
        grad_co = dot_tn(c_mixed, grad_branch)
        grad_q, grad_k, grad_v = attend_back(
            c_query, c_key, c_value, c_weight, low(dot_nt(grad_branch, co))
        )
        grad_cq = dot_tn(c_normed, grad_q)
        grad_text, grad_gain_q = norm_back(text_y, gain_q, dot_nt(grad_q, cq))
        grad_keyval = jnp.concatenate([grad_k, grad_v], axis=1)
        grad_ckv = dot_tn(image_normed, grad_keyval)
        grad_image, grad_gain_i = norm_back(image_in, gain_i, dot_nt(grad_keyval, ckv))
        cross_sums = jnp.stack(
            [
                squares(c_branch, row_weight),
                squares(c_mlp, row_weight),
                squares(final_rows, row_weight),
            ]
        )
        grads = tuple(low(g) for g in (grad_cq, grad_ckv, grad_co, grad_cu))
        grad_ca = jnp.stack(
            [
                jnp.concatenate([g[:, h * n : (h + 1) * n] for g, n in zip(grads, cuts)], axis=1)
                for h in range(2)
            ]
        )
        return (
            low(final_rows),
            grad_middle + grad_text,
            low(grad_image),
            grad_ca,
            low(grad_cd),
            jnp.concatenate([grad_gain_q, grad_gain_i, grad_gain_c]),
            cross_sums,
        )

    def skip_cross(operands):
        shapes = jax.eval_shape(run_cross, operands)
        return tuple(jnp.zeros(s.shape, s.dtype) for s in shapes)

    final_rows, grad_text, grad_image, grad_ca, grad_cd, grad_cross_gains, cross_sums = lax.cond(
        decoder, run_cross, skip_cross, (layer_y, arrived)
    )
    returned = lax.ppermute(grad_image, "tower", [(1, 0)]).astype(f32)
    grad_top = jnp.where(decoder, grad_text, upstream + returned)

    grad_middle, grad_gain_2, grad_up, grad_down = mlp_back(
        middle, gain_2, up, down, mlp_stored, grad_top
    )
    grad_branch = low(grad_middle)
    grad_out = dot_tn(mixed, grad_branch)
    grad_joined = jnp.concatenate(
        attend_back(query, key, value, weight, low(dot_nt(grad_branch, out))), axis=1
    )
    grad_qkv = dot_tn(normed, grad_joined)
    grad_stream, grad_gain_1 = norm_back(stream, gain_1, dot_nt(grad_joined, qkv))
    grad_stream = grad_middle + grad_stream

    layer_sums = jnp.stack(
        [
            squares(stream, row_weight),
            squares(attn_branch, row_weight),
            squares(mlp_branch, row_weight),
            squares(layer_y, row_weight),
        ]
    )
    encoder_part = jnp.where(decoder, 0.0, layer_sums)
    decoder_part = jnp.where(decoder, jnp.concatenate([layer_sums[:3], cross_sums]), 0.0)
    counted = jnp.where(decoder, jnp.sum(valid_rows.astype(f32)), 0.0)
    line = tile_row(jnp.concatenate([encoder_part, decoder_part, counted[None]]))
    self_gains = jnp.concatenate([grad_gain_1, grad_gain_2])
    zero = jnp.zeros_like(self_gains)
    vec = jnp.concatenate(
        [
            jnp.where(decoder, zero, self_gains),
            jnp.where(decoder, self_gains, zero),
            grad_cross_gains,
            line,
        ]
    ).reshape(-1, 128)
    vec = jnp.pad(vec, ((0, -vec.shape[0] % 8), (0, 0)))
    grad_a = jnp.concatenate([low(grad_qkv), low(grad_out), low(grad_up)], axis=1)
    chips = 2 * lines
    partial_sums = (
        grad_a.reshape(chips, 2, rows, -1),
        low(grad_down).reshape(chips, 2, -1, width),
        grad_ca.reshape(2, 2, chips, 2 * few, -1),
        grad_cd.reshape(2, chips, 2, -1, width),
        vec,
    )
    if fills:
        results = scatter(lines, *partial_sums, self_parts, cuts)
    else:
        results = plain_scatter(*partial_sums, self_parts, cuts)
    o_qkv, o_out, o_up, o_d, o_cq, o_ckv, o_co, o_cu, o_cd, o_vec = results
    flat = o_vec.reshape(-1)
    own_gains = lax.dynamic_slice(flat, (tower * 2 * width,), (2 * width,))
    g_1, g_2 = (lax.dynamic_slice(own_gains, (i * width + dp * rows,), (rows,)) for i in range(2))
    g_q, g_i, g_c = (
        lax.dynamic_slice(
            flat, ((4 + i) * width + (tower * dp_count + dp) * few,), (few,)
        )
        for i in range(3)
    )
    sums = flat[7 * width : 7 * width + 11]
    encoder_count = jnp.full((4,), float(row_count * dp_count), f32)
    divisor = jnp.concatenate([encoder_count, jnp.full((6,), 1.0, f32) * sums[10]]) * width
    rms_values = jnp.sqrt(sums[:10] / divisor)
    layer_out = jnp.where(decoder, final_rows, image_rows)
    return (
        layer_out[None], grad_stream[None], g_1[None], o_qkv[None], o_out[None], g_2[None],
        o_up[None], o_d[None], g_q, g_i, g_c, o_cq, o_ckv, o_co, o_cu, o_cd, rms_values,
    )


def solution(mesh):
    rows = P("tower", "dp", None)
    gain = P("tower", "dp")
    cross_gain = P(("tower", "dp"))
    cross = P(("tower", "dp"), None)
    weights = (gain, rows, rows, gain, rows, rows) + (cross_gain,) * 3 + (cross,) * 5
    return jax.shard_map(
        shards,
        mesh=mesh,
        in_specs=(rows, rows, P("dp", None), P("dp")) + weights,
        out_specs=(rows, rows) + weights + (P(),),
        check_vma=False,
    )
```

time: 1680 us -> 522 us (0.31)
  waiting for transfers between devices: 1130 us -> 95 us
  Pallas kernels: 0 us -> 291 us
  blocking collectives: 174 us -> 0 us
  local copies, waits for them, and re-layouts: 146 us -> 34.7 us
  matrix products: 114 us -> 47.3 us
  starting transfers between devices: 41 us -> 7.03 us
    unnamed x13 -> x0, waiting for transfers between devices: 629 us -> none
    all_gather x9 -> x0, waiting for transfers between devices: 338 us -> none  [the longest x1 65.3 us: shards(): lax.all_gather(cross_up, ('tower', 'dp'), axis=0, tiled=True)]
    pallas_call x0 -> x2, Pallas kernels: none -> 291 us  [the longest x1 151 us: scatter(): pl.pallas_call(functools.partial(scatter_kernel, lines, wide, cuts), out_...]
    unnamed x3 -> x0, blocking collectives: 138 us -> none
    dot_general x96 -> x17, matrix products: 114 us -> 44.9 us  [the longest x4 14.6 us: dot_nt(): return jnp.einsum('re,de->rd', a, b, preferred_element_type=jnp.float32)]
    ppermute x2, waiting for transfers between devices: 161 us -> 95 us  [the longest x1 88.8 us: shards(): returned = lax.ppermute(grad_image, 'tower', [(1, 0)]).astype(f32)]
    reshape x18 -> x2, local copies, waits for them, and re-layouts: 52.9 us -> 7.61 us  [the longest x1 4.92 us: shards(): grad_ca.reshape(2, 2, chips, 2 * few, -1)]
    squeeze x1 -> x0, blocking collectives: 35.2 us -> none  [shards(): layer_weights = tuple((member[0] for member in gathered))]
  transfers between devices with their start and end apart: 13 -> 2, of which waited for: 9 -> 2; matrix products, arithmetic and copies ran while one was open for 14% -> 1% of each run, Pallas kernels for 0% -> 0%
where the time goes in v1:
time: 522 us; the launch traced here: 512 us
  Pallas kernels  291 us (56%)
  waiting for transfers between devices  95 us (18%)
  matrix products  47.3 us (9%)
  local copies, waits for them, and re-layouts  34.7 us (7%)
  other arithmetic  26.7 us (5%)
  loops' own time  8.64 us (2%)
  starting transfers between devices  7.03 us (1%)
    pallas_call x1, Pallas kernels, scatter(): pl.pallas_call(functools.partial(scatter_kernel, lines, wide, cuts), out_...  151 us
    pallas_call x1, Pallas kernels, gather(): pl.pallas_call(functools.partial(gather_kernel, lines, wide, width), out_...  140 us
    ppermute x1, waiting for transfers between devices, shards(): returned = lax.ppermute(grad_image, 'tower', [(1, 0)]).astype(f32)  88.8 us
    dot_general x4, matrix products, dot_nt(): return jnp.einsum('re,de->rd', a, b, preferred_element_type=jnp.float32)  14.6 us
    unnamed x89, local copies, waits for them, and re-layouts  14.2 us
    dot_general x4, matrix products, dot_tn(): return jnp.einsum('rd,re->de', a, b, preferred_element_type=jnp.float32)  13 us
    dot_general x4, matrix products, dot(): return jnp.dot(a, b, preferred_element_type=jnp.float32)  11.6 us
  transfers between devices with their start and end apart: 2, of which 2 were waited for; matrix products, arithmetic and copies ran while one was open for 1% of the time, Pallas kernels for 0%

profile of v1, /device:TPU:0, one launch (start us, length us, event | category | flops | bytes accessed | tf_op | source)
XLA Modules:
  0.0 512.4 jit_solution(8131390904936802218)
XLA Ops:
  7.3 139.9 %shard_map.305 = (bf16[768,6144]{1,0:T(8,128)(2,1)S(1)}, bf16[3072,768]{1,0:T(8,128)(2,1)S(1)}, bf16[2,768,3072]{2,1,0:T(8,128)(2,1)}, bf16[3072,768]{1,0:T(8,128)(2,1)}, f32[2,16,8,128]{3,2,1,0:T(8,128)S(1)}) custom-call(bf16[48,6144]{1,0:T(8,128)(2,1)S(1)} %pad_maximum_fusion.22.own_a, bf16[192,768]{1,0:T(8,128)(2,1)S(1)} %bitcast.178, ...), custom_call_target="tpu_custom_call" | custom-call | tf_op jit(solution)/shard_map/pallas_call | solution.py:285
  147.2 3.6 copy-done
  150.8 2.2 copy-done.3
  153.5 2.9 convolution_convert_fusion.13
  158.4 2.4 fusion.144
  162.8 2.7 fusion.128
  165.8 3.6 fusion.63
  169.5 2.3 fusion.127
  171.9 5.7 %collective-permute-start = (bf16[192,768]{1,0:T(8,128)(2,1)S(1)}, bf16[192,768]{1,0:T(8,128)(2,1)S(1)}, u32[]{:S(2)}, u32[]{:S(2)}) collective-permute-start(bf16[192,768]{1,0:T(8,128)(2,1)S(1)} %get-tuple-element.134), channel_id=1, source_target_pairs={{0,16},{1,17},{2,18},{3,19},{4,20},{5,21},{6,22},{7,23},{8,24},{9,... | collective-permute-start | bytes 884744 | tf_op jit(solution)/shard_map/ppermute | solution.py:865
  178.5 6.2 %collective-permute-done = bf16[192,768]{1,0:T(8,128)(2,1)S(1)} collective-permute-done((bf16[192,768]{1,0:T(8,128)(2,1)S(1)}, bf16[192,768]{1,0:T(8,128)(2,1)S(1)}, u32[]{:S(2)}, u32[]{:S(2)}) %collective-permute-start) | collective-permute-done | bytes 294944 | tf_op jit(solution)/shard_map/ppermute | solution.py:865
  184.7 18.6 %conditional.1 = (bf16[192,768]{1,0:T(8,128)(2,1)}, f32[192,768]{1,0:T(8,128)}, bf16[192,768]{1,0:T(8,128)(2,1)}, f32[2304]{0:T(1024)S(1)}, f32[3]{0:T(128)S(1)}...) conditional(s32[]{:T(128)} %convert_element_type.235, () %tuple.20, ...), branch_computations={%region_9.10_spmd, %region_10.32_spmd} | conditional | flops 8629313536 | bytes 330304960 | solution.py:928
  184.7 4.9 reshape.417
  189.6 2.7 reshape.418
  207.1 88.8 %collective-permute-done.1 = bf16[192,768]{1,0:T(8,128)(2,1)S(1)} collective-permute-done((bf16[192,768]{1,0:T(8,128)(2,1)}, bf16[192,768]{1,0:T(8,128)(2,1)S(1)}, u32[]{:S(2)}, u32[]{:S(2)}) %collective-permute-start.1) | collective-permute-done | bytes 294944 | tf_op jit(solution)/shard_map/ppermute | solution.py:931
  296.0 4.8 fusion.74
  300.8 4.6 multiply_reduce_fusion.8
  307.9 2.4 multiply_reduce_fusion.7
  313.8 4.3 convolution_convert_fusion.11
  318.1 3.4 fusion.95
  321.6 3.2 convolution_convert_fusion.10
  326.3 3.9 convolution_convert_fusion.12
  331.5 2.7 broadcast_select_fusion.1
  338.5 9.1 %pad_maximum_fusion.20 = bf16[768,6144]{1,0:T(8,128)(2,1)} fusion(bf16[768,3072]{1,0:T(8,128)(2,1)} %convolution_convert_fusion.12, bf16[768,768]{1,0:T(8,128)(2,1)S(1)} %copy.105, bf16[768,2304]{1,0:T(8,128)(2,1)} %convolution_convert_fusion.10), kind=kLoop, calls=%fused_computation.124 | loop fusion | flops 28311552 | bytes 18874368 | tf_op jit(solution)/shard_map/concatenate | solution.py:969
  347.6 150.7 %shard_map.306 = (f32[48,2304]{1,0:T(8,128)}, f32[48,768]{1,0:T(8,128)}, f32[48,3072]{1,0:T(8,128)}, f32[192,768]{1,0:T(8,128)}, f32[24,768]{1,0:T(8,128)}, /*in...) custom-call(bf16[8,2,48,6144]{3,2,1,0:T(8,128)(2,1)} %bitcast.181, ...), custom_call_target="tpu_custom_call" | custom-call | tf_op jit(solution)/shard_map/pallas_call | solution.py:661
  (159 shorter events, 44.4 us)
Async XLA Ops:
  0.7 6.6 %copy-start.1 = (bf16[1,192,768]{2,1,0:T(8,128)(2,1)S(1)}, bf16[1,192,768]{2,1,0:T(8,128)(2,1)}, u32[]{:S(2)}) copy-start(bf16[1,192,768]{2,1,0:T(8,128)(2,1)} %param.29) | copy-start | bytes 884740
  0.7 6.6 %copy-start.2 = (bf16[96,768]{1,0:T(8,128)(2,1)S(1)}, bf16[96,768]{1,0:T(8,128)(2,1)}, u32[]{:S(2)}) copy-start(bf16[96,768]{1,0:T(8,128)(2,1)} %own_cd.1) | copy-start | bytes 442372
  2.5 150.7 %copy-start.5 = (bf16[1,192,768]{2,1,0:T(8,128)(2,1)S(1)}, bf16[1,192,768]{2,1,0:T(8,128)(2,1)}, u32[]{:S(2)}) copy-start(bf16[1,192,768]{2,1,0:T(8,128)(2,1)} %param.20) | copy-start | bytes 884740
  158.2 4.6 copy-start.51
  162.8 6.6 %copy-start.36 = (bf16[12,64,192]{2,1,0:T(8,128)(2,1)}, bf16[12,64,192]{2,1,0:T(8,128)(2,1)S(1)}, u32[]{:S(2)}) copy-start(bf16[12,64,192]{2,1,0:T(8,128)(2,1)S(1)} %convolution_convert_fusion.16) | copy-start | bytes 884740
  162.8 6.7 %slice-start = ((s8[4718592]{0:T(1024)(128)(4,1)}), s8[524288]{0:T(1024)(128)(4,1)S(1)}, s32[]{:S(2)}) async-start(s8[4718592]{0:T(1024)(128)(4,1)} %bitcast.179), calls=%async_computation | async-start | bytes 1048576
  169.5 8.1 %copy-start.12 = (bf16[1,192,768]{2,1,0:T(8,128)(2,1)S(1)}, bf16[1,192,768]{2,1,0:T(8,128)(2,1)}, u32[]{:S(2)}) copy-start(bf16[1,192,768]{2,1,0:T(8,128)(2,1)} %param.21) | copy-start | bytes 884740
  171.9 12.9 %copy-start.57 = (bf16[192,768]{1,0:T(8,128)(2,1)}, bf16[192,768]{1,0:T(8,128)(2,1)S(1)}, u32[]{:S(2)}) copy-start(bf16[192,768]{1,0:T(8,128)(2,1)S(1)} %get-tuple-element.134) | copy-start | bytes 884740
  171.9 12.8 %collective-permute-start = (bf16[192,768]{1,0:T(8,128)(2,1)S(1)}, bf16[192,768]{1,0:T(8,128)(2,1)S(1)}, u32[]{:S(2)}, u32[]{:S(2)}) collective-permute-start(bf16[192,768]{1,0:T(8,128)(2,1)S(1)} %get-tuple-element.134), channel_id=1, source_target_pairs={{0,16},{1,17},{2,18},{3,19},{4,20},{5,21},{6,22},{7,23},{8,24},{9,... | collective-permute-start | bytes 884744 | tf_op jit(solution)/shard_map/ppermute | solution.py:865
  184.7 111.2 %copy-start.13 = (bf16[1,192,768]{2,1,0:T(8,128)(2,1)S(1)}, bf16[1,192,768]{2,1,0:T(8,128)(2,1)}, u32[]{:S(2)}) copy-start(bf16[1,192,768]{2,1,0:T(8,128)(2,1)} %param.21) | copy-start | bytes 884740
  203.3 92.6 %collective-permute-start.1 = (bf16[192,768]{1,0:T(8,128)(2,1)}, bf16[192,768]{1,0:T(8,128)(2,1)S(1)}, u32[]{:S(2)}, u32[]{:S(2)}) collective-permute-start(bf16[192,768]{1,0:T(8,128)(2,1)} %get-tuple-element.83), channel_id=1, source_target_pairs={{16,0},{17,1},{18,2},{19,3},{20,4},{21,5},{22,6},{23,7},{24,8},{25... | collective-permute-start | bytes 884744 | tf_op jit(solution)/shard_map/ppermute | solution.py:931
  205.3 90.8 %copy-start.68 = (f32[192,3072]{1,0:T(8,128)S(1)}, f32[192,3072]{1,0:T(8,128)}, u32[]{:S(2)}) copy-start(f32[192,3072]{1,0:T(8,128)} %copy-done.67) | copy-start | bytes 7077892
  300.8 4.6 copy-start.39
  321.6 8.7 %copy-start.23 = (f32[192,768]{1,0:T(8,128)}, f32[192,768]{1,0:T(8,128)S(1)}, u32[]{:S(2)}) copy-start(f32[192,768]{1,0:T(8,128)S(1)} %get-tuple-element.192) | copy-start | bytes 1769476
  347.6 152.1 %copy-start.24 = (f32[192,768]{1,0:T(8,128)S(1)}, f32[192,768]{1,0:T(8,128)}, u32[]{:S(2)}) copy-start(f32[192,768]{1,0:T(8,128)} %copy-done.23) | copy-start | bytes 1769476
  498.3 7.2 %copy-start.50 = (f32[48,2304]{1,0:T(8,128)S(1)}, f32[48,2304]{1,0:T(8,128)}, u32[]{:S(2)}) copy-start(f32[48,2304]{1,0:T(8,128)} %get-tuple-element.89) | copy-start | bytes 1327108
  498.3 7.9 %copy-start.61 = (f32[48,768]{1,0:T(8,128)S(1)}, f32[48,768]{1,0:T(8,128)}, u32[]{:S(2)}) copy-start(f32[48,768]{1,0:T(8,128)} %get-tuple-element.90) | copy-start | bytes 442372
  498.3 8.6 %copy-start.47 = (f32[48,3072]{1,0:T(8,128)S(1)}, f32[48,3072]{1,0:T(8,128)}, u32[]{:S(2)}) copy-start(f32[48,3072]{1,0:T(8,128)} %get-tuple-element.91) | copy-start | bytes 1769476
  498.3 9.4 %copy-start.46 = (f32[192,768]{1,0:T(8,128)S(1)}, f32[192,768]{1,0:T(8,128)}, u32[]{:S(2)}) copy-start(f32[192,768]{1,0:T(8,128)} %get-tuple-element.92) | copy-start | bytes 1769476
  499.7 8.8 %copy-start.63 = (f32[24,768]{1,0:T(8,128)S(1)}, f32[24,768]{1,0:T(8,128)}, u32[]{:S(2)}) copy-start(f32[24,768]{1,0:T(8,128)} %get-tuple-element.243) | copy-start | bytes 221188
  500.8 8.4 %copy-start.60 = (f32[24,1536]{1,0:T(8,128)S(1)}, f32[24,1536]{1,0:T(8,128)}, u32[]{:S(2)}) copy-start(f32[24,1536]{1,0:T(8,128)} %get-tuple-element.244) | copy-start | bytes 442372
  500.8 9.1 %copy-start.62 = (f32[24,768]{1,0:T(8,128)S(1)}, f32[24,768]{1,0:T(8,128)}, u32[]{:S(2)}) copy-start(f32[24,768]{1,0:T(8,128)} %get-tuple-element.245) | copy-start | bytes 221188
  500.8 9.7 %copy-start.59 = (f32[24,3072]{1,0:T(8,128)S(1)}, f32[24,3072]{1,0:T(8,128)}, u32[]{:S(2)}) copy-start(f32[24,3072]{1,0:T(8,128)} %get-tuple-element.246) | copy-start | bytes 884740
  505.5 5.7 %copy-start.58 = (f32[96,768]{1,0:T(8,128)S(1)}, f32[96,768]{1,0:T(8,128)}, u32[]{:S(2)}) copy-start(f32[96,768]{1,0:T(8,128)} %get-tuple-element.247) | copy-start | bytes 884740
  (18 other events, 47.4 us)

commit v2 on v1

--- a/solution.py
+++ b/solution.py
@@ -201,283 +201,6 @@
             when(net.text, all_of(0, 0))
 
 
-def gather_kernel(
-    lines, wide, half, own_a, own_d, pack, own_cd, own_g, full_a, full_d, full_ca, full_cd, full_g,
-    swap, block, send_sem, recv_sem, local_sem, swap_sem,
-):
-    net = Net(lines)
-    net.barrier()
-    rows, depth = own_a.shape[0], own_d.shape[0]
-    few, part = pack.shape[1], own_cd.shape[0]
-    swapped = net.copy("core", pack.at[1 - net.core], swap, swap_sem.at[0], swap_sem.at[1])
-    swapped.start()
-
-    def columns(first, last):
-        return lambda tower, chip, core: full_a.at[
-            pl.ds(pl.multiple_of((2 * chip + core) * rows, rows), rows), first:last
-        ]
-
-    def plan(index, own, place, crossing, everywhere=False):
-        return Gather(
-            net, own, place, crossing, send_sem.at[index], recv_sem.at[index], local_sem.at[index], everywhere
-        )
-
-    jobs = [
-        plan(0, own_g, lambda tower, chip, core: full_g.at[tower, 2 * chip + core], True, True),
-        plan(1, own_a.at[:, 0:wide], columns(0, wide), False),
-        plan(2, own_a.at[:, wide:], columns(wide, own_a.shape[1]), False),
-        plan(
-            3,
-            own_d,
-            lambda tower, chip, core: full_d.at[
-                pl.ds(pl.multiple_of((2 * chip + core) * depth, depth), depth), :
-            ],
-            False,
-        ),
-        plan(
-            4,
-            block,
-            lambda tower, chip, core: full_ca.at[
-                core, pl.ds(pl.multiple_of((tower * 2 * lines + chip) * 2 * few, 2 * few), 2 * few), :
-            ],
-            True,
-        ),
-        plan(
-            5,
-            own_cd,
-            lambda tower, chip, core: full_cd.at[
-                pl.ds(
-                    pl.multiple_of((tower * 4 * lines + 2 * chip + core) * part, part), part
-                ),
-                :,
-            ],
-            True,
-        ),
-    ]
-    for job in jobs[:4]:
-        job.start()
-    swapped.wait()
-    first = net.core == 0
-    mine = pack[net.core]
-    theirs = swap[...]
-    block[0:few] = jnp.where(first, mine, theirs).astype(jnp.bfloat16)
-    block[few:] = jnp.where(first, theirs, mine).astype(jnp.bfloat16)
-    for job in jobs[4:]:
-        job.start()
-    for job in jobs:
-        job.beside(0)
-        job.from_image(0)
-    for k in range(1, lines):
-        for job in jobs:
-            job.hop(k)
-        for job in jobs:
-            job.beside(k)
-            job.from_image(k)
-    for job in jobs:
-        job.done()
-    net.finish()
-
-
-def gather(lines, wide, own_a, own_d, pack, own_cd, own_g):
-    count = 4 * lines
-    half, few, width = pack.shape
-    jobs = 6
-    return pl.pallas_call(
-        functools.partial(gather_kernel, lines, wide, width),
-        out_shape=(
-            jax.ShapeDtypeStruct((count * own_a.shape[0], own_a.shape[1]), jnp.bfloat16),
-            jax.ShapeDtypeStruct((count * own_d.shape[0], own_d.shape[1]), jnp.bfloat16),
-            jax.ShapeDtypeStruct((2, 2 * count * few, width), jnp.bfloat16),
-            jax.ShapeDtypeStruct((2 * count * own_cd.shape[0], own_cd.shape[1]), jnp.bfloat16),
-            jax.ShapeDtypeStruct((2, count) + own_g.shape, jnp.float32),
-        ),
-        in_specs=[ANY, ANY, VMEM, ANY, ANY],
-        out_specs=[ANY] * 5,
-        scratch_shapes=[
-            pltpu.VMEM((few, width), jnp.float32),
-            pltpu.VMEM((2 * few, width), jnp.bfloat16),
-            pltpu.SemaphoreType.DMA((jobs, Gather.sems(lines))),
-            pltpu.SemaphoreType.DMA((jobs, Gather.sems(lines))),
-            pltpu.SemaphoreType.DMA((jobs,)),
-            pltpu.SemaphoreType.DMA((2,)),
-        ],
-        compiler_params=pltpu.CompilerParams(
-            collective_id=0, has_side_effects=True, vmem_limit_bytes=32 << 20
-        ),
-    )(own_a, own_d, pack, own_cd, own_g)
-
-
-class Scatter:
-    def __init__(self, net, crossing, grad, own, beside, near, far, sems):
-        self.net, self.crossing, self.grad = net, crossing, grad
-        self.own, self.rcv, self.near, self.far = own, beside, near, far
-        self.send_sem, self.recv_sem, self.local_sem = sems
-
-    def add(self, pairs, out):
-        shape = out.shape
-        step = 16
-
-        def one(i, carry):
-            rows = pl.ds(pl.multiple_of(i * step, step), step)
-            total = pairs[0][rows, :].astype(jnp.float32)
-            for other in pairs[1:]:
-                total = total + other[rows, :].astype(jnp.float32)
-            out[rows, :] = total.astype(out.dtype)
-            return carry
-
-        lax.fori_loop(0, shape[0] // step, one, 0)
-
-    @staticmethod
-    def sems(lines):
-        return 1 + 5 * lines
-
-    def plane(self):
-        return self.own.at[self.net.tower] if self.crossing else self.own
-
-    def start(self):
-        net = self.net
-        there = net.text if self.crossing else None
-        self.load = pltpu.make_async_copy(self.grad(net.core), self.own, self.local_sem)
-        when(there, self.load.start)
-        net.send(
-            "core", self.grad(1 - net.core), self.rcv, self.send_sem.at[0], self.recv_sem.at[0], there
-        )
-
-    def chips(self, k):
-        net = self.net
-        if k == 0:
-            return ((None, net.z),)
-        return (
-            (net.z + k < net.lines, jnp.minimum(net.z + k, net.lines - 1)),
-            (net.z >= k, jnp.maximum(net.z - k, 0)),
-        )
-
-    def cores(self):
-        net = self.net
-        lines = net.lines
-        there = net.text if self.crossing else None
-
-        def arrived():
-            self.load.wait()
-
-        when(there, arrived)
-        net.arrive(self.rcv, self.send_sem.at[0], self.recv_sem.at[0], there)
-
-        def sum_of(own, rcv):
-            def one(i, carry):
-                self.add([own.at[i], rcv.at[i]], own.at[i])
-                return carry
-
-            lax.fori_loop(0, 2 * lines, one, 0)
-
-        if self.crossing:
-
-            def text():
-                sum_of(self.own.at[0], self.rcv.at[0])
-
-            when(there, text)
-            for k in range(lines - 1, -1, -1):
-                for there_k, z in self.chips(k):
-                    for y in (1 - net.y, net.y):
-                        chip = 2 * z + y
-                        s = 1 + chip
-                        net.send(
-                            "x",
-                            self.own.at[0, chip],
-                            self.own.at[0, chip],
-                            self.send_sem.at[s],
-                            self.recv_sem.at[s],
-                            both(there_k, net.text),
-                        )
-
-            def text_too():
-                sum_of(self.own.at[1], self.rcv.at[1])
-
-            when(there, text_too)
-        else:
-            sum_of(self.own, self.rcv)
-
-    def across(self):
-        net = self.net
-        lines = net.lines
-        for k in range(lines - 1, -1, -1):
-            for there, z in self.chips(k):
-                chip = 2 * z + 1 - net.y
-                if self.crossing:
-                    s = 1 + chip
-                    net.arrive(
-                        self.own.at[0, chip],
-                        self.send_sem.at[s],
-                        self.recv_sem.at[s],
-                        both(there, net.image),
-                    )
-                s = 1 + 2 * lines + z
-                net.send(
-                    "y", self.plane().at[chip], self.near.at[z], self.send_sem.at[s], self.recv_sem.at[s], there
-                )
-
-    def along(self):
-        net = self.net
-        lines = net.lines
-        own = self.plane()
-        for k in range(lines - 1, 0, -1):
-            for way, (there, z) in zip(("up", "down"), self.chips(k)):
-                chip = 2 * z + net.y
-                up = way == "up"
-                base = 1 + 3 * lines if up else 1 + 4 * lines
-                if self.crossing:
-                    s = 1 + chip
-                    net.arrive(
-                        self.own.at[0, chip],
-                        self.send_sem.at[s],
-                        self.recv_sem.at[s],
-                        both(there, net.image),
-                    )
-                s = 1 + 2 * lines + z
-                net.arrive(self.near.at[z], self.send_sem.at[s], self.recv_sem.at[s], there)
-                more = net.low if up else net.high
-                s = base + z
-                net.arrive(self.far.at[z], self.send_sem.at[s], self.recv_sem.at[s], both(there, more))
-
-                def with_far():
-                    self.add([own.at[chip], self.near.at[z], self.far.at[z]], own.at[chip])
-
-                def without():
-                    self.add([own.at[chip], self.near.at[z]], own.at[chip])
-
-                when(both(there, more), with_far)
-                when(both(there, jnp.logical_not(more)), without)
-                slot = z
-                if up:
-                    target = self.far.at[slot]
-                else:
-                    last = jnp.where(z == net.z - 1, lines, z)
-                    target = self.far.at[last]
-                net.send(way, own.at[chip], target, self.send_sem.at[s], self.recv_sem.at[s], there)
-
-    def total(self, out):
-        net = self.net
-        lines = net.lines
-        own = self.plane()
-        chip = net.chip
-        if self.crossing:
-            s = 1 + chip
-            net.arrive(
-                self.own.at[0, chip], self.send_sem.at[s], self.recv_sem.at[s], net.image
-            )
-        s = 1 + 2 * lines + net.z
-        net.arrive(self.near.at[net.z], self.send_sem.at[s], self.recv_sem.at[s])
-        s = 1 + 3 * lines + net.z
-        net.arrive(self.far.at[net.z], self.send_sem.at[s], self.recv_sem.at[s], net.low)
-        s = 1 + 4 * lines + net.z
-        net.arrive(self.far.at[lines], self.send_sem.at[s], self.recv_sem.at[s], net.high)
-        here = [own.at[chip], self.near.at[net.z]]
-        from_low, from_high = self.far.at[net.z], self.far.at[lines]
-        when(both(net.low, net.high), lambda: self.add(here + [from_low, from_high], out))
-        when(jnp.logical_not(net.low), lambda: self.add(here + [from_high], out))
-        when(jnp.logical_not(net.high), lambda: self.add(here + [from_low], out))
-
-
 class Small:
     def __init__(self, net, mine, arrived, sums, wide, send_sem, recv_sem):
         self.net, self.mine, self.arrived, self.sums, self.wide = net, mine, arrived, sums, wide
@@ -522,85 +245,1001 @@
         out[...] = total
 
 
-def scatter_kernel(
-    lines, wide, cuts, g_a, g_d, g_ca, g_cd, vec,
-    o_qkv, o_out, o_up, o_d, o_cq, o_ckv, o_co, o_cu, o_cd, o_vec,
-    *scratch,
+def product(a, b, axis_a=1, axis_b=0):
+    return lax.dot_general(
+        a, b, (((axis_a,), (axis_b,)), ((), ())), preferred_element_type=jnp.float32
+    )
+
+
+def low(value):
+    return value.astype(jnp.bfloat16)
+
+
+def blocks(count, size, body):
+    def one(i, carry):
+        body(pl.ds(pl.multiple_of(i * size, size), size))
+        return carry
+
+    lax.fori_loop(0, count // size, one, 0)
+
+
+def row_step(rows):
+    return next(s for s in (96, 64, 48, 32, 16) if rows % s == 0)
+
+
+def centred(value):
+    center = value - jnp.mean(value, axis=-1, keepdims=True)
+    spread = jnp.mean(center * center, axis=-1, keepdims=True)
+    return center * lax.rsqrt(spread + EPSILON), lax.rsqrt(spread + EPSILON)
+
+
+def norm_rows(src, gain, out, also=None):
+    def body(rows):
+        value = src[rows, :].astype(jnp.float32)
+        if also is not None:
+            also(rows, value)
+        out[rows, :] = low(centred(value)[0] * gain)
+
+    blocks(src.shape[0], row_step(src.shape[0]), body)
+
+
+def norm_back_rows(src, gain, grad, done, gain_grad):
+    gain_grad[...] = jnp.zeros_like(gain_grad)
+
+    def body(rows):
+        n, scale = centred(src[rows, :].astype(jnp.float32))
+        out = grad[rows, :]
+        dn = out * gain
+        gain_grad[...] += jnp.sum(out * n, axis=0, keepdims=True)
+        back = dn - jnp.mean(dn, axis=-1, keepdims=True)
+        done(rows, (back - n * jnp.mean(dn * n, axis=-1, keepdims=True)) * scale)
+
+    blocks(src.shape[0], row_step(src.shape[0]), body)
+
+
+class Sums:
+    def __init__(self, ref, weight):
+        self.ref, self.weight = ref, weight
+        ref[...] = jnp.zeros_like(ref)
+
+    def add(self, slot, rows, value):
+        kept = jnp.sum(value * value, axis=-1, keepdims=True) * self.weight[rows, :]
+        total = jnp.sum(kept, axis=0, keepdims=True)
+        at = pl.ds(slot, 1)
+        self.ref[at, :] = self.ref[at, :] + jnp.broadcast_to(total, (1, self.ref.shape[1]))
+
+    def line(self):
+        shape = self.ref.shape
+        row = lax.broadcasted_iota(jnp.int32, shape, 0)
+        lane = lax.broadcasted_iota(jnp.int32, shape, 1)
+        return jnp.sum(jnp.where(row == lane, self.ref[...], 0.0), axis=0, keepdims=True)
+
+
+def pair_count(width):
+    pairs = width // (2 * HD)
+    return next(n for n in (3, 2, 1) if pairs % n == 0)
+
+
+def attention(query, key, value, allowed, weight, mixed):
+    count, width = mixed.shape
+    group = pair_count(width)
+    left = lax.broadcasted_iota(jnp.int32, (count, 2 * HD), 1) < HD
+
+    def one(step, carry):
+        kept, scores = [], []
+        for i in range(group):
+            pair = step * group + i
+            q, k, v = query(pair), key(pair), value(pair)
+            zero = jnp.zeros_like(q)
+            kept.append((pair, v))
+            for part in (jnp.where(left, q, zero), jnp.where(left, zero, q)):
+                scores.append(product(part, k, 1, 1) * HD ** (-0.5))
+        weights = []
+        for s in scores:
+            s = jnp.where(allowed[...] > 0, s, NEGATIVE)
+            e = jnp.exp(s - jnp.max(s, axis=-1, keepdims=True))
+            weights.append(low(e / jnp.sum(e, axis=-1, keepdims=True)))
+        for i, (pair, v) in enumerate(kept):
+            first, second = weights[2 * i : 2 * i + 2]
+            weight[2 * pair] = first
+            weight[2 * pair + 1] = second
+            both_heads = jnp.where(left, product(first, v), product(second, v))
+            mixed[:, pl.ds(pl.multiple_of(pair * 2 * HD, 2 * HD), 2 * HD)] = low(both_heads)
+        return carry
+
+    lax.fori_loop(0, width // (2 * HD) // group, one, 0)
+
+
+def attention_back(query, key, value, grad_mixed, weight, width, done):
+    count = weight.shape[1]
+    group = pair_count(width)
+    left = lax.broadcasted_iota(jnp.int32, (count, 2 * HD), 1) < HD
+
+    def one(step, carry):
+        kept, raw = [], []
+        for i in range(group):
+            pair = step * group + i
+            q, k, v, d = query(pair), key(pair), value(pair), grad_mixed(pair)
+            zero = jnp.zeros_like(q)
+            kept.append((pair, q, k))
+            for h, part in enumerate((jnp.where(left, d, zero), jnp.where(left, zero, d))):
+                raw.append((part, product(part, v, 1, 1), weight[2 * pair + h]))
+        grads = []
+        for part, dp, p in raw:
+            p32 = p.astype(jnp.float32)
+            grads.append(low(p32 * (dp - jnp.sum(dp * p32, axis=-1, keepdims=True))))
+        for i, (pair, q, k) in enumerate(kept):
+            (d0, _, p0), (d1, _, p1) = raw[2 * i : 2 * i + 2]
+            s0, s1 = grads[2 * i : 2 * i + 2]
+            zero = jnp.zeros_like(q)
+            dv = product(p0, d0, 0, 0) + product(p1, d1, 0, 0)
+            dk = product(s0, jnp.where(left, q, zero), 0, 0)
+            dk = dk + product(s1, jnp.where(left, zero, q), 0, 0)
+            dq = jnp.where(left, product(s0, k), product(s1, k))
+            done(pair, low(dq * HD ** (-0.5)), low(dk * HD ** (-0.5)), low(dv))
+        return carry
+
+    lax.fori_loop(0, width // (2 * HD) // group, one, 0)
+
+
+def pairs_of(ref, base=0):
+    return lambda pair: ref[:, pl.ds(pl.multiple_of(base + pair * 2 * HD, 2 * HD), 2 * HD)]
+
+
+def gelu_both(value):
+    scale = 0.7978845608028654
+    cube = 0.044715
+    square = value * value
+    bend = jnp.tanh(scale * value * (1.0 + cube * square))
+    half = 0.5 * (1.0 + bend)
+    slope = half + 0.5 * value * (1.0 - bend * bend) * scale * (1.0 + 3.0 * cube * square)
+    return value * half, slope
+
+
+def activate(wide, active, slope, columns):
+    def body(rows):
+        a, s = gelu_both(wide[rows, :])
+        active[rows, columns] = low(a)
+        slope[rows, columns] = s.astype(slope.dtype)
+
+    blocks(wide.shape[0], 16, body)
+
+
+def forward_kernel(
+    lines, cuts, parts,
+    tok, cot, allowed, cross_allowed, row_weight, gvec, own_a, own_d, pack, own_cd,
+    full_a, full_d, sum_ca, sum_cd, o_h1, o_qkv, o_mixed, o_weight, o_middle, o_h2, o_active, o_slope,
+    gains, layer_out, top, vec,
+    w_a, w_d, w_ca, w_cd, h1, qkv, mixed, weight, middle, h2, active, slope, out_y, wide, branch,
+    passed, image_out, n_q, n_i, query, keyval, c_mixed, c_weight, c_middle, h3, grad_wide, g_small,
+    swap, block, rcv_a, rcv_d, arrived, totals, spread, sums_ref, gain_rows,
+    send_sem, recv_sem, local_sem, swap_sem, s_send, s_recv, pass_sem, out_sem, d_send, d_recv, d_local,
 ):
     net = Net(lines)
     net.barrier()
-    buffers = [scratch[4 * i : 4 * i + 4] for i in range(5)]
-    send_sem, recv_sem, local_sem, fin, swap, swap_sem, arrived, sums, spread, s_send, s_recv = scratch[20:]
-    small = Small(net, vec, arrived, sums, spread, s_send, s_recv)
-    width = g_ca.shape[-1]
-    few = g_ca.shape[-2]
-
-    def job(index, crossing, grad):
-        return Scatter(
-            net,
-            crossing,
-            grad,
-            *buffers[index],
-            (send_sem.at[index], recv_sem.at[index], local_sem.at[index]),
-        )
-
-    s_d = job(0, False, lambda core: g_d.at[:, core])
-    c_d = job(1, True, lambda core: g_cd.at[:, :, core])
-    s_up = job(2, False, lambda core: g_a.at[:, core, :, pl.ds(wide, g_a.shape[-1] - wide)])
-    c_a = job(3, True, lambda core: g_ca.at[core])
-    s_qkv = job(4, False, lambda core: g_a.at[:, core, :, pl.ds(0, wide)])
-
+    text, image = net.text, net.image
+    rows, depth = own_a.shape[0], own_d.shape[0]
+    few, part = pack.shape[1], own_cd.shape[0]
+    width = tok.shape[1]
+    half = pack.shape[2]
+    a_qkv, a_out = parts[0], parts[0] + parts[1]
+    q_end, kv_end, o_end = cuts[0], cuts[0] + cuts[1], cuts[0] + cuts[1] + cuts[2]
+    tile = width
+
+    def columns(first, last):
+        return lambda tower, chip, core: w_a.at[
+            pl.ds(pl.multiple_of((2 * chip + core) * rows, rows), rows), first:last
+        ]
+
+    def crossed(first, last):
+        return lambda tower, chip, core: w_ca.at[
+            core,
+            pl.ds(pl.multiple_of((tower * 2 * lines + chip) * 2 * few, 2 * few), 2 * few),
+            first:last,
+        ]
+
+    def plan(index, own, place, crossing):
+        return Gather(
+            net, own, place, crossing, send_sem.at[index], recv_sem.at[index], local_sem.at[index]
+        )
+
+    j_qkv = plan(0, own_a.at[:, 0:a_qkv], columns(0, a_qkv), False)
+    j_out = plan(1, own_a.at[:, a_qkv:a_out], columns(a_qkv, a_out), False)
+    j_up = plan(2, own_a.at[:, a_out:], columns(a_out, own_a.shape[1]), False)
+    j_down = plan(
+        3,
+        own_d,
+        lambda tower, chip, core: w_d.at[
+            pl.ds(pl.multiple_of((2 * chip + core) * depth, depth), depth), :
+        ],
+        False,
+    )
+    j_att = plan(4, block.at[:, 0:o_end], crossed(0, o_end), True)
+    j_cup = plan(5, block.at[:, o_end:], crossed(o_end, half), True)
+    j_cdown = plan(
+        6,
+        own_cd,
+        lambda tower, chip, core: w_cd.at[
+            pl.ds(pl.multiple_of((tower * 4 * lines + 2 * chip + core) * part, part), part), :
+        ],
+        True,
+    )
+    kept = []
+
+    def keep(src, dst):
+        copy = pltpu.make_async_copy(src, dst, out_sem.at[len(kept)])
+        copy.start()
+        kept.append(copy)
+
+    swapped = net.copy("core", pack.at[1 - net.core], swap, swap_sem.at[0], swap_sem.at[1])
+    swapped.start()
+    small = Small(net, gvec, arrived, totals, spread, s_send, s_recv)
     small.exchange(0)
-    s_d.start()
-    c_d.start()
-    s_d.cores()
-    s_d.across()
-    s_up.start()
+    j_qkv.start()
+    j_out.start()
+    swapped.wait()
+    first = net.core == 0
+    mine = pack[net.core]
+    theirs = swap[...]
+    block[0:few] = low(jnp.where(first, mine, theirs))
+    block[few:] = low(jnp.where(first, theirs, mine))
     small.collect(0)
     small.exchange(1)
-    c_d.cores()
-    c_a.start()
-    s_d.along()
-    s_up.cores()
-    s_qkv.start()
-    c_d.across()
-    s_up.across()
+    j_qkv.beside(0)
     small.collect(1)
     small.exchange(2)
-    c_a.cores()
-    c_d.along()
-    s_qkv.cores()
-    s_d.total(o_d)
-    c_a.across()
-    s_qkv.across()
+    j_qkv.hop(1)
+    j_qkv.beside(1)
     small.collect(2)
     small.spread()
-    s_up.along()
+    j_qkv.hop(2)
+    j_qkv.beside(2)
+    j_up.start()
+    small.total(gains)
+    sums = Sums(sums_ref, row_weight)
+    gain_rows[...] = jnp.zeros_like(gain_rows)
+    base = 4 * net.tower
+
+    def gain(at):
+        return jnp.where(text, gains[at + 2 : at + 3, :], gains[at : at + 1, :])
+
+    norm_rows(tok, gain(0), h1, lambda r, v: sums.add(base, r, v))
+    for k in range(3, lines):
+        j_qkv.hop(k)
+        j_qkv.beside(k)
+    j_qkv.done()
+
+    def qkv_tile(cols):
+        qkv[:, cols] = low(product(h1[...], w_a[:, cols]))
+
+    blocks(a_qkv, tile, qkv_tile)
+    keep(h1, o_h1)
+
+    def step(job, follow):
+        job.beside(0)
+        job.from_image(0)
+        for k in range(1, lines):
+            if k == lines - 1 and follow is not None:
+                follow.start()
+            job.hop(k)
+            job.beside(k)
+            job.from_image(k)
+        job.done()
+
+    step(j_out, None)
+    attention(
+        pairs_of(qkv), pairs_of(qkv, width), pairs_of(qkv, 2 * width), allowed, weight, mixed
+    )
+    keep(qkv, o_qkv)
+    keep(weight, o_weight)
+    keep(mixed, o_mixed)
+    branch[...] = product(mixed[...], w_a[:, a_qkv:a_out])
+
+    def add_branch(r):
+        value = branch[r, :]
+        sums.add(base + 1, r, value)
+        middle[r, :] = tok[r, :].astype(jnp.float32) + value
+
+    blocks(tok.shape[0], row_step(tok.shape[0]), add_branch)
+    keep(middle, o_middle)
+    norm_rows(middle, gain(1), h2)
+    keep(h2, o_h2)
+    step(j_up, j_down)
+
+    def up_tile(i, carry):
+        at = pl.multiple_of(i * tile, tile)
+        wide[...] = product(h2[...], w_a[:, pl.ds(a_out + at, tile)])
+        activate(wide, active, slope, pl.ds(at, tile))
+        return carry
+
+    lax.fori_loop(0, active.shape[1] // tile, up_tile, 0)
+    keep(active, o_active)
+    keep(slope, o_slope)
+    keep(w_a, full_a)
+    step(j_down, j_att)
+    keep(w_d, full_d)
+    branch[...] = product(active[...], w_d[...])
+
+    def add_mlp(r):
+        value = branch[r, :]
+        sums.add(base + 2, r, value)
+        y = middle[r, :] + value
+        out_y[r, :] = y
+        image_out[r, :] = low(y)
+
+        @pl.when(image)
+        def _():
+            sums.add(3, r, y)
+
+    blocks(tok.shape[0], row_step(tok.shape[0]), add_mlp)
+    net.send("x", image_out, passed, pass_sem.at[0], pass_sem.at[1], image)
+    step(j_att, j_cup)
+
+    @pl.when(text)
+    def _():
+        norm_rows(out_y, gains[4:5, :], n_q)
+        for h in range(2):
+            at = h * cuts[0]
+            query[:, at : at + cuts[0]] = low(product(n_q[...], w_ca[h, :, 0:q_end]))
+
+    step(j_cup, j_cdown)
+    net.arrive(passed, pass_sem.at[0], pass_sem.at[1], text)
+    step(j_cdown, None)
+
+    net.finish()
+    for copy in kept:
+        copy.wait()
+    def hand(index, src, rcv, there=text):
+        net.send("core", src, rcv, d_send.at[index], d_recv.at[index], there)
+
+    def merge(index, own, rcv, out):
+        net.arrive(rcv, d_send.at[index], d_recv.at[index], text)
+
+        @pl.when(text)
+        def _():
+            def add(r):
+                rcv[r, :] = low(own[r, :].astype(jnp.float32) + rcv[r, :].astype(jnp.float32))
+
+            blocks(rcv.shape[0], 16, add)
+            pltpu.make_async_copy(rcv, out, d_local.at[index]).start()
+
+    @pl.when(text)
+    def _():
+        norm_rows(passed, gains[5:6, :], n_i)
+        for h in range(2):
+            at = h * width
+            keyval[:, at : at + width] = low(product(n_i[...], w_ca[h, :, q_end:kv_end]))
+        attention(
+            pairs_of(query), pairs_of(keyval), pairs_of(keyval, width), cross_allowed, c_weight, c_mixed
+        )
+        for h in range(2):
+            at = h * cuts[2]
+            branch[:, at : at + cuts[2]] = product(c_mixed[...], w_ca[h, :, kv_end:o_end])
+
+        def add_cross(r):
+            value = branch[r, :]
+            sums.add(7, r, value)
+            c_middle[r, :] = out_y[r, :] + value
+
+        blocks(tok.shape[0], row_step(tok.shape[0]), add_cross)
+        norm_rows(c_middle, gains[6:7, :], h3)
+
+        for h in range(2):
+
+            def cross_up(i, carry):
+                at = pl.multiple_of(i * tile, tile)
+                wide[...] = product(h3[...], w_ca[h, :, pl.ds(o_end + at, tile)])
+                activate(wide, active, slope, pl.ds(h * cuts[3] + at, tile))
+                return carry
+
+            lax.fori_loop(0, cuts[3] // tile, cross_up, 0)
+        branch[...] = product(active[...], w_cd[...])
+
+        def add_final(r):
+            value = branch[r, :]
+            sums.add(8, r, value)
+            z = c_middle[r, :] + value
+            sums.add(9, r, z)
+            layer_out[r, :] = low(z)
+
+        blocks(tok.shape[0], row_step(tok.shape[0]), add_final)
+
+        def down_tile(i, carry):
+            cols = pl.ds(pl.multiple_of(i * tile, tile), tile)
+            found = low(product(active[:, cols], cot[...], 0, 0))
+            for k in range(tile // part):
+                at = (k % 2) * (w_d.shape[0] // 2) + (k // 2) * part + i * (tile // 2)
+                w_d[pl.ds(pl.multiple_of(at, part), part), :] = found[k * part : (k + 1) * part]
+            grad = product(cot[...], w_cd[cols, :], 1, 1)
+            grad_wide[:, cols] = low(grad * slope[:, cols])
+            return carry
+
+        lax.fori_loop(0, active.shape[1] // tile, down_tile, 0)
+
+    share = w_d.shape[0] // 2
+    hand(0, w_d.at[pl.ds(pl.multiple_of((1 - net.core) * share, share), share), :], rcv_d)
+
+    @pl.when(text)
+    def _():
+        for h in range(2):
+
+            def up_grad(i, carry):
+                at = pl.multiple_of(i * tile, tile)
+                w_a[:, pl.ds(h * half + o_end + at, tile)] = low(
+                    product(h3[...], grad_wide[:, pl.ds(h * cuts[3] + at, tile)], 0, 0)
+                )
+                return carry
+
+            lax.fori_loop(0, cuts[3] // tile, up_grad, 0)
+
+    theirs_at = pl.multiple_of((1 - net.core) * half, half)
+    mine_at = pl.multiple_of(net.core * half, half)
+    hand(1, w_a.at[:, pl.ds(theirs_at + o_end, half - o_end)], rcv_a.at[:, o_end:half])
+
+    @pl.when(text)
+    def _():
+        branch[...] = product(grad_wide[:, 0 : cuts[3]], w_ca[0, :, o_end:half], 1, 1) + product(
+            grad_wide[:, cuts[3] :], w_ca[1, :, o_end:half], 1, 1
+        )
+
+        def mid_done(r, back):
+            total = cot[r, :].astype(jnp.float32) + back
+            c_middle[r, :] = total
+            h3[r, :] = low(total)
+
+        norm_back_rows(c_middle, gains[6:7, :], branch, mid_done, g_small)
+        gain_rows[6:7, :] = g_small[...]
+        for h in range(2):
+            at = h * cuts[2]
+            w_a[:, h * half + kv_end : h * half + o_end] = low(
+                product(c_mixed[...], h3[:, at : at + cuts[2]], 0, 0)
+            )
+        branch[...] = product(h3[:, 0 : cuts[2]], w_ca[0, :, kv_end:o_end], 1, 1) + product(
+            h3[:, cuts[2] :], w_ca[1, :, kv_end:o_end], 1, 1
+        )
+        c_mixed[...] = low(branch[...])
+
+        def att_done(pair, dq, dk, dv):
+            at = pl.multiple_of(pair * 2 * HD, 2 * HD)
+            query[:, pl.ds(at, 2 * HD)] = dq
+            keyval[:, pl.ds(at, 2 * HD)] = dk
+            keyval[:, pl.ds(width + at, 2 * HD)] = dv
+
+        attention_back(
+            pairs_of(query),
+            pairs_of(keyval),
+            pairs_of(keyval, width),
+            pairs_of(c_mixed),
+            c_weight,
+            width,
+            att_done,
+        )
+        branch[...] = product(keyval[:, 0:width], w_ca[0, :, q_end:kv_end], 1, 1) + product(
+            keyval[:, width:], w_ca[1, :, q_end:kv_end], 1, 1
+        )
+
+        def image_done(r, back):
+            image_out[r, :] = low(back)
+
+        norm_back_rows(passed, gains[5:6, :], branch, image_done, g_small)
+        gain_rows[5:6, :] = g_small[...]
+
+    net.send("x", image_out, passed, pass_sem.at[0], pass_sem.at[1], text)
+
+    @pl.when(text)
+    def _():
+        for h in range(2):
+            at = h * width
+            w_a[:, h * half + q_end : h * half + kv_end] = low(
+                product(n_i[...], keyval[:, at : at + width], 0, 0)
+            )
+            at = h * cuts[0]
+            w_a[:, h * half : h * half + q_end] = low(
+                product(n_q[...], query[:, at : at + cuts[0]], 0, 0)
+            )
+
+    hand(2, w_a.at[:, pl.ds(theirs_at, o_end)], rcv_a.at[:, 0:o_end])
+    mine_d = w_d.at[pl.ds(pl.multiple_of(net.core * share, share), share), :]
+    merge(0, mine_d, rcv_d, sum_cd)
+    merge(
+        1,
+        w_a.at[:, pl.ds(mine_at + o_end, half - o_end)],
+        rcv_a.at[:, o_end:half],
+        sum_ca.at[:, o_end:half],
+    )
+
+    @pl.when(text)
+    def _():
+        branch[...] = product(query[:, 0 : cuts[0]], w_ca[0, :, 0:q_end], 1, 1) + product(
+            query[:, cuts[0] :], w_ca[1, :, 0:q_end], 1, 1
+        )
+
+        def text_done(r, back):
+            top[r, :] = c_middle[r, :] + back
+
+        norm_back_rows(out_y, gains[4:5, :], branch, text_done, g_small)
+        gain_rows[4:5, :] = g_small[...]
+        sums_ref[10:11, :] = jnp.broadcast_to(
+            jnp.sum(row_weight[...], axis=0, keepdims=True), (1, sums_ref.shape[1])
+        )
+        vec[...] = gain_rows[...]
+
+    merge(2, w_a.at[:, pl.ds(mine_at, o_end)], rcv_a.at[:, 0:o_end], sum_ca.at[:, 0:o_end])
+    net.arrive(passed, pass_sem.at[0], pass_sem.at[1], image)
+
+    @pl.when(image)
+    def _():
+        vec[...] = jnp.zeros_like(vec)
+
+        def add_back(r):
+            top[r, :] = cot[r, :].astype(jnp.float32) + passed[r, :].astype(jnp.float32)
+            layer_out[r, :] = image_out[r, :]
+
+        blocks(tok.shape[0], row_step(tok.shape[0]), add_back)
+
+    vec[7:8, 0 : sums_ref.shape[1]] = sums.line()
+
+    @pl.when(text)
+    def _():
+        for index, (src, out) in enumerate(
+            (
+                (rcv_d, sum_cd),
+                (rcv_a.at[:, o_end:half], sum_ca.at[:, o_end:half]),
+                (rcv_a.at[:, 0:o_end], sum_ca.at[:, 0:o_end]),
+            )
+        ):
+            pltpu.make_async_copy(src, out, d_local.at[index]).wait()
+
+    net.finish()
+
+
+def forward(lines, cuts, parts, *operands):
+    tok, cot, allowed, cross_allowed, row_weight, gvec, own_a, own_d, pack, own_cd = operands
+    bf16, f32 = jnp.bfloat16, jnp.float32
+    count = 4 * lines
+    rows, width = tok.shape
+    few, half = pack.shape[1:]
+    hidden = count * own_d.shape[0]
+    all_a = (count * own_a.shape[0], own_a.shape[1])
+    heads_n = width // HD
+    jobs = 7
+    shape = jax.ShapeDtypeStruct
+    wide_b, wide_f = (rows, width), (rows, hidden)
+    stored = [
+        (wide_b, bf16),
+        ((rows, parts[0]), bf16),
+        (wide_b, bf16),
+        ((heads_n, rows, rows), bf16),
+        (wide_b, f32),
+        (wide_b, bf16),
+        (wide_f, bf16),
+        (wide_f, f32),
+    ]
+    outs = [
+        (all_a, bf16),
+        ((hidden, width), bf16),
+        ((width, half), bf16),
+        ((hidden // 2, width), bf16),
+        *stored,
+        (gvec.shape, f32),
+        (wide_b, bf16),
+        (wide_b, f32),
+        (gvec.shape, f32),
+    ]
+    scratch = [
+        (all_a, bf16),
+        ((hidden, width), bf16),
+        ((2, width, half), bf16),
+        ((hidden, width), bf16),
+        *stored,
+        (wide_b, f32),
+        (wide_b, f32),
+        (wide_b, f32),
+        (wide_b, bf16),
+        (wide_b, bf16),
+        (wide_b, bf16),
+        (wide_b, bf16),
+        (wide_b, bf16),
+        ((rows, 2 * width), bf16),
+        (wide_b, bf16),
+        ((heads_n, rows, rows), bf16),
+        (wide_b, f32),
+        (wide_b, bf16),
+        (wide_f, bf16),
+        ((1, width), f32),
+        ((few, half), f32),
+        ((2 * few, half), bf16),
+        ((width, half), bf16),
+        ((hidden // 2, width), bf16),
+        ((3,) + gvec.shape, f32),
+        ((3,) + gvec.shape, f32),
+        ((lines - 1,) + gvec.shape, f32),
+        ((16, 128), f32),
+        (gvec.shape, f32),
+    ]
+    dma = pltpu.SemaphoreType.DMA
+    return pl.pallas_call(
+        functools.partial(forward_kernel, lines, cuts, parts),
+        out_shape=tuple(shape(*o) for o in outs),
+        in_specs=[VMEM] * 6 + [ANY, ANY, VMEM, ANY],
+        out_specs=[ANY] * 12 + [VMEM] * 4,
+        scratch_shapes=[pltpu.VMEM(*s) for s in scratch]
+        + [
+            dma((jobs, Gather.sems(lines))),
+            dma((jobs, Gather.sems(lines))),
+            dma((jobs,)),
+            dma((2,)),
+            dma((2 + lines,)),
+            dma((2 + lines,)),
+            dma((2,)),
+            dma((12,)),
+            dma((3,)),
+            dma((3,)),
+            dma((3,)),
+        ],
+        compiler_params=pltpu.CompilerParams(
+            collective_id=0, has_side_effects=True, vmem_limit_bytes=63 << 20
+        ),
+    )(*operands)
+
+
+class Scatter:
+    def __init__(self, net, own, near, far, rcv, sems):
+        self.net, self.own, self.near, self.far, self.rcv = net, own, near, far, rcv
+        self.send_sem, self.recv_sem = sems
+
+    @staticmethod
+    def sems(lines):
+        return 1 + 5 * lines
+
+    def sem(self, s):
+        return self.send_sem.at[s], self.recv_sem.at[s]
+
+    def add(self, pairs, out):
+        def one(r):
+            total = pairs[0][r, :].astype(jnp.float32)
+            for other in pairs[1:]:
+                total = total + other[r, :].astype(jnp.float32)
+            out[r, :] = total.astype(out.dtype)
+
+        blocks(out.shape[0], 16, one)
+
+    def chips(self, k):
+        net = self.net
+        if k == 0:
+            return ((None, net.z),)
+        return (
+            (net.z + k < net.lines, jnp.minimum(net.z + k, net.lines - 1)),
+            (net.z >= k, jnp.maximum(net.z - k, 0)),
+        )
+
+    def order(self):
+        return [pair for k in range(self.net.lines - 1, -1, -1) for pair in self.chips(k)]
+
+    def swap(self, theirs, rcv):
+        self.whole = rcv
+        self.net.send("core", theirs, rcv, *self.sem(0))
+
+    def swapped(self):
+        self.net.arrive(self.whole, *self.sem(0))
+
+    def over_x(self, part):
+        net = self.net
+        for there, z in self.order():
+            for y in (1 - net.y, net.y):
+                chip = 2 * z + y
+                net.send("x", part(chip), self.own(chip), *self.sem(1 + chip), both(there, net.text))
+
+    def from_x(self, chip, there):
+        if self.rcv is None:
+            net = self.net
+            net.arrive(self.own(chip), *self.sem(1 + chip), both(there, net.image))
+
+    def across(self, only=None):
+        net = self.net
+        for there, z in self.order():
+            there = both(there, only)
+            chip = 2 * z + 1 - net.y
+            self.from_x(chip, there)
+            own = self.own(chip)
+            if self.rcv is not None:
+                when(there, lambda: self.add([own, self.rcv(chip)], own))
+            net.send("y", own, self.near(z), *self.sem(1 + 2 * net.lines + z), there)
+
+    def here(self, chip, z):
+        parts = [self.own(chip), self.near(z)]
+        return parts if self.rcv is None else parts + [self.rcv(chip)]
+
+    def along(self, k):
+        net = self.net
+        lines = net.lines
+        for up, (there, z) in zip((True, False), self.chips(k)):
+            chip = 2 * z + net.y
+            base = (1 + 3 * lines) if up else (1 + 4 * lines)
+            self.from_x(chip, there)
+            net.arrive(self.near(z), *self.sem(1 + 2 * lines + z), there)
+            more = net.low if up else net.high
+            s = base + z
+            net.arrive(self.far(z), *self.sem(s), both(there, more))
+            own = self.own(chip)
+            parts = self.here(chip, z)
+            when(both(there, more), lambda: self.add(parts + [self.far(z)], own))
+            when(both(there, jnp.logical_not(more)), lambda: self.add(parts, own))
+            slot = z if up else jnp.where(z == net.z - 1, lines, z)
+            net.send("up" if up else "down", own, self.far(slot), *self.sem(s), there)
+
+    def total(self, out):
+        net = self.net
+        lines = net.lines
+        self.from_x(net.chip, None)
+        net.arrive(self.near(net.z), *self.sem(1 + 2 * lines + net.z))
+        net.arrive(self.far(net.z), *self.sem(1 + 3 * lines + net.z), net.low)
+        net.arrive(self.far(lines), *self.sem(1 + 4 * lines + net.z), net.high)
+        parts = self.here(net.chip, net.z)
+        low_part, high_part = self.far(net.z), self.far(lines)
+        when(both(net.low, net.high), lambda: self.add(parts + [low_part, high_part], out))
+        when(jnp.logical_not(net.low), lambda: self.add(parts + [high_part], out))
+        when(jnp.logical_not(net.high), lambda: self.add(parts + [low_part], out))
+
+
+def strip(ref, size, first, last):
+    return lambda i: ref.at[pl.ds(pl.multiple_of(i * size, size), size), first:last]
+
+
+def backward_kernel(
+    lines, cuts, parts,
+    tok, top_in, gains, vec_in, full_a, full_d, sum_ca, sum_cd,
+    i_h1, i_qkv, i_mixed, i_weight, i_middle, i_h2, i_active, i_slope,
+    o_qkv, o_out, o_up, o_d, o_cq, o_ckv, o_co, o_cu, o_cd, input_grad, o_vec,
+    h1, qkv, mixed, weight, middle, h2, active, slope,
+    g_a, g_d, rcv_a, rcv_d, near_a, near_d, far_a, far_d,
+    own_ca, own_cd, near_ca, near_cd, far_ca, far_cd,
+    w_d, w_up, top, branch, n_grad, g_small, vec, fin, swap, arrived, totals, spread,
+    send_sem, recv_sem, load_sem, swap_sem, s_send, s_recv,
+):
+    net = Net(lines)
+    net.barrier()
+    text, image = net.text, net.image
+    width = tok.shape[1]
+    tile = width
+    rows, depth = o_qkv.shape[0], o_d.shape[0]
+    few, part = 2 * o_cq.shape[0], o_cd.shape[0]
+    half = own_ca.shape[1]
+    a_out = parts[0] + parts[1]
+    all_a = g_a.shape[2]
+    o_end = cuts[0] + cuts[1] + cuts[2]
+    theirs = 1 - net.core
+
+    def load(index, src, dst):
+        copy = pltpu.make_async_copy(src, dst, load_sem.at[index])
+        copy.start()
+        return copy
+
+    l_active = load(0, i_active, active)
+    l_wd = load(1, full_d, w_d)
+    l_slope = load(2, i_slope, slope)
+    l_h2 = load(3, i_h2, h2)
+    l_up = load(4, full_a.at[:, a_out:], w_up)
+    l_middle = load(5, i_middle, middle)
+    l_mixed = load(6, i_mixed, mixed)
+    l_qkv = load(7, i_qkv, qkv)
+    l_weight = load(8, i_weight, weight)
+    l_h1 = load(9, i_h1, h1)
+
+    def job(index, own, near, far, rcv):
+        return Scatter(net, own, near, far, rcv, (send_sem.at[index], recv_sem.at[index]))
+
+    def self_a(index, first, last):
+        return job(
+            index,
+            strip(g_a.at[net.core], rows, first, last),
+            strip(near_a, rows, first, last),
+            strip(far_a, rows, first, last),
+            strip(rcv_a, rows, first, last),
+        )
+
+    def cross_a(index, first, last):
+        return job(
+            index,
+            strip(own_ca, few, first, last),
+            strip(near_ca, few, first, last),
+            strip(far_ca, few, first, last),
+            None,
+        )
+
+    s_d = job(
+        0,
+        strip(g_d.at[net.core], depth, 0, width),
+        strip(near_d, depth, 0, width),
+        strip(far_d, depth, 0, width),
+        strip(rcv_d, depth, 0, width),
+    )
+    s_up = self_a(1, a_out, all_a)
+    s_att = self_a(2, 0, a_out)
+    c_d = job(
+        3,
+        strip(own_cd, part, 0, width),
+        strip(near_cd, part, 0, width),
+        strip(far_cd, part, 0, width),
+        None,
+    )
+    c_up = cross_a(4, o_end, half)
+    c_att = cross_a(5, 0, o_end)
+
+    plane_a, plane_d = own_ca.shape[0], own_cd.shape[0]
+    c_loads = (
+        pltpu.make_async_copy(sum_cd.at[plane_d : 2 * plane_d, :], own_cd, load_sem.at[10]),
+        pltpu.make_async_copy(sum_ca.at[plane_a : 2 * plane_a, :], own_ca, load_sem.at[11]),
+    )
+
+    @pl.when(text)
+    def _():
+        for copy in c_loads:
+            copy.start()
+
+    c_d.over_x(strip(sum_cd, part, 0, width))
+    c_up.over_x(strip(sum_ca, few, o_end, half))
+    c_att.over_x(strip(sum_ca, few, 0, o_end))
+
+    def copy_top(r):
+        n_grad[r, :] = low(top_in[r, :])
+
+    blocks(tok.shape[0], row_step(tok.shape[0]), copy_top)
+
+    @pl.when(text)
+    def _():
+        for copy in c_loads:
+            copy.wait()
+
+    c_d.across(text)
+    l_active.wait()
+    l_wd.wait()
+    l_slope.wait()
+
+    def down_tile(i, carry):
+        cols = pl.ds(pl.multiple_of(i * tile, tile), tile)
+        found = low(product(active[:, cols], n_grad[...], 0, 0))
+        each = tile // depth
+        for k in range(each):
+            at = pl.multiple_of(((i * each + k) // 2) * depth, depth)
+            g_d[k % 2, pl.ds(at, depth), :] = found[k * depth : (k + 1) * depth]
+        grad = product(n_grad[...], w_d[cols, :], 1, 1)
+        active[:, cols] = low(grad * slope[:, cols])
+        return carry
+
+    lax.fori_loop(0, active.shape[1] // tile, down_tile, 0)
+    s_d.swap(g_d.at[theirs], rcv_d)
+    l_four = [
+        load(12 + i, full_a.at[:, i * width : (i + 1) * width], w_d.at[i * width : (i + 1) * width, :])
+        for i in range(4)
+    ]
+    l_h2.wait()
+
+    def put_a(found, at):
+        for k in range(width // rows):
+            g_a[k % 2, (k // 2) * rows : (k // 2 + 1) * rows, pl.ds(at, found.shape[1])] = found[
+                k * rows : (k + 1) * rows
+            ]
+
+    def up_tile(i, carry):
+        at = pl.multiple_of(i * tile, tile)
+        put_a(low(product(h2[...], active[:, pl.ds(at, tile)], 0, 0)), pl.multiple_of(a_out + at, tile))
+        return carry
+
+    lax.fori_loop(0, (all_a - a_out) // tile, up_tile, 0)
+    s_up.swap(g_a.at[theirs, :, a_out:all_a], rcv_a.at[:, a_out:all_a])
+    s_d.swapped()
+    s_d.across()
+    l_up.wait()
+    branch[...] = product(active[...], w_up[...], 1, 1)
+    l_middle.wait()
+
+    def mid_done(r, back):
+        total = top_in[r, :] + back
+        top[r, :] = total
+        n_grad[r, :] = low(total)
+
+    def own_gain(at):
+        return jnp.where(text, gains[at + 2 : at + 3, :], gains[at : at + 1, :])
+
+    norm_back_rows(middle, own_gain(1), branch, mid_done, g_small)
+    vec[...] = vec_in[...]
+    at_vec = 2 * net.tower
+    vec[pl.ds(at_vec + 1, 1), :] = g_small[...]
+    s_up.swapped()
+    s_up.across()
+    l_mixed.wait()
+    for copy in l_four:
+        copy.wait()
+    put_a(low(product(mixed[...], n_grad[...], 0, 0)), parts[0])
+    mixed[...] = low(product(n_grad[...], w_d[3 * width : 4 * width, :], 1, 1))
+    l_qkv.wait()
+    l_weight.wait()
+
+    def att_done(pair, dq, dk, dv):
+        at = pl.multiple_of(pair * 2 * HD, 2 * HD)
+        for k, grad in enumerate((dq, dk, dv)):
+            qkv[:, pl.ds(pl.multiple_of(k * width + at, 2 * HD), 2 * HD)] = grad
+
+    attention_back(
+        pairs_of(qkv),
+        pairs_of(qkv, width),
+        pairs_of(qkv, 2 * width),
+        pairs_of(mixed),
+        weight,
+        width,
+        att_done,
+    )
+    l_h1.wait()
+
+    def qkv_tile(i, carry):
+        at = pl.multiple_of(i * tile, tile)
+        put_a(low(product(h1[...], qkv[:, pl.ds(at, tile)], 0, 0)), at)
+        return carry
+
+    lax.fori_loop(0, parts[0] // tile, qkv_tile, 0)
+    s_att.swap(g_a.at[theirs, :, 0:a_out], rcv_a.at[:, 0:a_out])
+    branch[...] = (
+        product(qkv[:, 0:width], w_d[0:width, :], 1, 1)
+        + product(qkv[:, width : 2 * width], w_d[width : 2 * width, :], 1, 1)
+        + product(qkv[:, 2 * width :], w_d[2 * width : 3 * width, :], 1, 1)
+    )
+
+    def first_done(r, back):
+        input_grad[r, :] = top[r, :] + back
+
+    norm_back_rows(tok, own_gain(0), branch, first_done, g_small)
+    vec[pl.ds(at_vec, 1), :] = g_small[...]
+    small = Small(net, vec, arrived, totals, spread, s_send, s_recv)
+    small.exchange(0)
+    s_att.swapped()
+    s_att.across()
+    small.collect(0)
+    small.exchange(1)
+    c_d.across(image)
+    small.collect(1)
+    small.exchange(2)
+    far_first = range(lines - 1, 0, -1)
+    for k in far_first:
+        s_d.along(k)
+    small.collect(2)
+    small.spread()
+    c_up.across()
+    s_d.total(o_d)
+    for k in far_first:
+        s_up.along(k)
+    small.total(o_vec)
+    for k in far_first:
+        c_d.along(k)
+    s_up.total(o_up)
+    c_att.across()
     c_d.total(o_cd)
-    c_a.along()
-    s_up.total(fin.at[0:few, 0 : g_a.shape[-1] - wide])
-    o_out[...] = fin[0:few, 0 : o_out.shape[1]]
-    o_up[...] = fin[0:few, o_out.shape[1] : g_a.shape[-1] - wide]
-    s_qkv.along()
-    c_a.total(fin.at[0:few, 0:width])
+    for k in far_first:
+        s_att.along(k)
+    for k in far_first:
+        c_up.along(k)
+    s_att.total(fin)
+    o_qkv[...] = fin[:, 0 : parts[0]]
+    o_out[...] = fin[:, parts[0] : a_out]
+    for k in far_first:
+        c_att.along(k)
+    c_up.total(fin.at[:, o_end:half])
+    c_att.total(fin.at[:, 0:o_end])
     share = few // 2
-    other = 1 - net.core
     swapped = net.copy(
         "core",
-        fin.at[pl.ds(pl.multiple_of(other * share, share), share), 0:width],
+        fin.at[pl.ds(pl.multiple_of(theirs * share, share), share), :],
         swap,
         swap_sem.at[0],
         swap_sem.at[1],
     )
     swapped.start()
-    s_qkv.total(o_qkv)
-    small.total(o_vec)
     swapped.wait()
-    mine = fin[pl.ds(pl.multiple_of(net.core * share, share), share), 0:width]
-    theirs = swap[...]
+    mine = fin[pl.ds(pl.multiple_of(net.core * share, share), share), :]
+    other = swap[...]
     first = net.core == 0
-    left = jnp.where(first, mine, theirs)
-    right = jnp.where(first, theirs, mine)
+    left = jnp.where(first, mine, other)
+    right = jnp.where(first, other, mine)
     at = 0
     for out, n in zip((o_cq, o_ckv, o_co, o_cu), cuts):
         out[:, 0:n] = left[:, at : at + n]
@@ -609,65 +1248,71 @@
     net.finish()
 
 
-def scatter(lines, g_a, g_d, g_ca, g_cd, vec, parts, cuts):
+def backward(lines, cuts, parts, own_shapes, *operands):
+    bf16, f32 = jnp.bfloat16, jnp.float32
+    tok, top, gains, vec, full_a, full_d, sum_ca, sum_cd = operands[:8]
+    stored = [(o.shape, o.dtype) for o in operands[8:]]
     chips = 2 * lines
-    wide = parts[0]
-    rows = g_a.shape[2]
-    few = g_ca.shape[3]
-    bf16, f32 = jnp.bfloat16, jnp.float32
-
-    def buffers(crossing, rows, n):
-        whole = ((2, chips, rows, n) if crossing else (chips, rows, n))
-        return [
-            pltpu.VMEM(whole, bf16),
-            pltpu.VMEM(whole, bf16),
-            pltpu.VMEM((lines, rows, n), bf16),
-            pltpu.VMEM((lines + 1, rows, n), bf16),
-        ]
-
-    scratch = (
-        buffers(False, g_d.shape[2], g_d.shape[3])
-        + buffers(True, g_cd.shape[3], g_cd.shape[4])
-        + buffers(False, rows, g_a.shape[3] - wide)
-        + buffers(True, few, g_ca.shape[4])
-        + buffers(False, rows, wide)
+    row_count, width = tok.shape
+    hidden, all_a = full_d.shape[0], full_a.shape[1]
+    half = sum_ca.shape[1]
+    rows, depth = width // (2 * chips), hidden // (2 * chips)
+    few, part = width // (2 * chips), hidden // (4 * chips)
+    outs = [*own_shapes, (row_count, width), vec.shape]
+    rcv_a, rcv_d = (chips * rows, all_a), (chips * depth, width)
+    own_ca, own_cd = (chips * few, half), (chips * part, width)
+
+    def line(size, count):
+        return (size * count, all_a), (depth * count, width)
+
+    scratch = [
+        *stored,
+        ((2,) + rcv_a, bf16),
+        ((2,) + rcv_d, bf16),
+        (rcv_a, bf16),
+        (rcv_d, bf16),
+        ((lines * rows, all_a), bf16),
+        ((lines * depth, width), bf16),
+        (((lines + 1) * rows, all_a), bf16),
+        (((lines + 1) * depth, width), bf16),
+        (own_ca, bf16),
+        (own_cd, bf16),
+        ((lines * few, half), bf16),
+        ((lines * part, width), bf16),
+        (((lines + 1) * few, half), bf16),
+        (((lines + 1) * part, width), bf16),
+        ((hidden, width), bf16),
+        ((width, hidden), bf16),
+        ((row_count, width), f32),
+        ((row_count, width), f32),
+        ((row_count, width), bf16),
+        ((1, width), f32),
+        (vec.shape, f32),
+        ((rows, half), f32),
+        ((few // 2, half), f32),
+        ((3,) + vec.shape, f32),
+        ((3,) + vec.shape, f32),
+        ((lines - 1,) + vec.shape, f32),
+    ]
+    dma = pltpu.SemaphoreType.DMA
+    return pl.pallas_call(
+        functools.partial(backward_kernel, lines, cuts, parts),
+        out_shape=tuple(jax.ShapeDtypeStruct(s, f32) for s in outs),
+        in_specs=[VMEM] * 4 + [ANY] * 12,
+        out_specs=[VMEM] * len(outs),
+        scratch_shapes=[pltpu.VMEM(*s) for s in scratch]
         + [
-            pltpu.SemaphoreType.DMA((5, Scatter.sems(lines))),
-            pltpu.SemaphoreType.DMA((5, Scatter.sems(lines))),
-            pltpu.SemaphoreType.DMA((5,)),
-            pltpu.VMEM((rows, max(g_a.shape[3] - wide, g_ca.shape[4])), f32),
-            pltpu.VMEM((few // 2, g_ca.shape[4]), f32),
-            pltpu.SemaphoreType.DMA((2,)),
-            pltpu.VMEM((3,) + vec.shape, f32),
-            pltpu.VMEM((3,) + vec.shape, f32),
-            pltpu.VMEM((lines - 1,) + vec.shape, f32),
-            pltpu.SemaphoreType.DMA((2 + lines,)),
-            pltpu.SemaphoreType.DMA((2 + lines,)),
-        ]
-    )
-    share = few // 2
-    outs = [
-        (rows, parts[0]),
-        (rows, parts[1]),
-        (rows, parts[2]),
-        (g_d.shape[2], g_d.shape[3]),
-        (share, 2 * cuts[0]),
-        (share, 2 * cuts[1]),
-        (share, 2 * cuts[2]),
-        (share, 2 * cuts[3]),
-        (g_cd.shape[3], g_cd.shape[4]),
-        vec.shape,
-    ]
-    return pl.pallas_call(
-        functools.partial(scatter_kernel, lines, wide, cuts),
-        out_shape=tuple(jax.ShapeDtypeStruct(s, f32) for s in outs),
-        in_specs=[ANY, ANY, ANY, ANY, VMEM],
-        out_specs=[VMEM] * len(outs),
-        scratch_shapes=scratch,
+            dma((6, Scatter.sems(lines))),
+            dma((6, Scatter.sems(lines))),
+            dma((16,)),
+            dma((2,)),
+            dma((2 + lines,)),
+            dma((2 + lines,)),
+        ],
         compiler_params=pltpu.CompilerParams(
-            collective_id=1, has_side_effects=True, vmem_limit_bytes=62 << 20
+            collective_id=1, has_side_effects=True, vmem_limit_bytes=63 << 20
         ),
-    )(g_a, g_d, g_ca, g_cd, vec)
+    )(*operands)
 
 
 def plain_gather(own_a, own_d, pack, own_cd, own_g):
@@ -802,7 +1447,7 @@
     return jnp.sum(row_weight[:, None] * value_matrix * value_matrix)
 
 
-def shards(
+def plain_shards(
     tokens, cotangent, kept_counts, caption_lengths, attn_gain, qkv_weight, attn_out, mlp_gain,
     mlp_up, mlp_down, query_gain, image_gain, cross_gain, cross_query, cross_keyval, cross_out,
     cross_up, cross_down,
@@ -834,11 +1479,9 @@
     ).astype(f32)
     self_parts = (qkv_weight.shape[2], attn_out.shape[2], mlp_up.shape[2])
     own_a = jnp.concatenate([qkv_weight[0], attn_out[0], mlp_up[0]], axis=1)
-    fills = dp_count % 4 == 0 and dp_count > 4 and rows % 16 == 0 and few % 8 == 0
-    fills = fills and cross_down.shape[0] % 16 == 0
-    own = (own_a, mlp_down[0], pack, cross_down, gain_tile)
-    full = gather(lines, self_parts[0], *own) if fills else plain_gather(*own)
-    full_a, full_d, full_ca, full_cd, full_g = full
+    full_a, full_d, full_ca, full_cd, full_g = plain_gather(
+        own_a, mlp_down[0], pack, cross_down, gain_tile
+    )
     qkv = full_a[:, : self_parts[0]]
     out = full_a[:, self_parts[0] : self_parts[0] + self_parts[1]]
     up = full_a[:, self_parts[0] + self_parts[1] :]
@@ -968,17 +1611,15 @@
     vec = jnp.pad(vec, ((0, -vec.shape[0] % 8), (0, 0)))
     grad_a = jnp.concatenate([low(grad_qkv), low(grad_out), low(grad_up)], axis=1)
     chips = 2 * lines
-    partial_sums = (
+    results = plain_scatter(
         grad_a.reshape(chips, 2, rows, -1),
         low(grad_down).reshape(chips, 2, -1, width),
         grad_ca.reshape(2, 2, chips, 2 * few, -1),
         grad_cd.reshape(2, chips, 2, -1, width),
         vec,
-    )
-    if fills:
-        results = scatter(lines, *partial_sums, self_parts, cuts)
-    else:
-        results = plain_scatter(*partial_sums, self_parts, cuts)
+        self_parts,
+        cuts,
+    )
     o_qkv, o_out, o_up, o_d, o_cq, o_ckv, o_co, o_cu, o_cd, o_vec = results
     flat = o_vec.reshape(-1)
     own_gains = lax.dynamic_slice(flat, (tower * 2 * width,), (2 * width,))
@@ -998,6 +1639,92 @@
         layer_out[None], grad_stream[None], g_1[None], o_qkv[None], o_out[None], g_2[None],
         o_up[None], o_d[None], g_q, g_i, g_c, o_cq, o_ckv, o_co, o_cu, o_cd, rms_values,
     )
+
+
+def fused_shards(
+    tokens, cotangent, kept_counts, caption_lengths, attn_gain, qkv_weight, attn_out, mlp_gain,
+    mlp_up, mlp_down, query_gain, image_gain, cross_gain, cross_query, cross_keyval, cross_out,
+    cross_up, cross_down,
+):
+    f32 = jnp.float32
+    dp_count = lax.axis_size("dp")
+    lines = dp_count // 4
+    tower, dp = lax.axis_index("tower"), lax.axis_index("dp")
+    decoder = tower == 1
+    row_count, width = tokens.shape[1:]
+    rows = attn_gain.shape[1]
+    few = query_gain.shape[0]
+    lane = jnp.arange(width)
+
+    def in_place(value, index):
+        n = value.shape[0]
+        return jnp.where(lane // n == index, jnp.tile(value.astype(f32), width // n), 0.0)
+
+    first, second = in_place(attn_gain[0], dp), in_place(mlp_gain[0], dp)
+    zero = jnp.zeros_like(first)
+    gvec = jnp.stack(
+        [
+            jnp.where(decoder, zero, first),
+            jnp.where(decoder, zero, second),
+            jnp.where(decoder, first, zero),
+            jnp.where(decoder, second, zero),
+        ]
+        + [in_place(g, tower * dp_count + dp) for g in (query_gain, image_gain, cross_gain)]
+        + [zero]
+    )
+    cross_shards = (cross_query, cross_keyval, cross_out, cross_up)
+    cuts = tuple(w.shape[1] // 2 for w in cross_shards)
+    pack = jnp.stack(
+        [
+            jnp.concatenate([w[:, h * n : (h + 1) * n] for w, n in zip(cross_shards, cuts)], axis=1)
+            for h in range(2)
+        ]
+    ).astype(f32)
+    parts = (qkv_weight.shape[2], attn_out.shape[2], mlp_up.shape[2])
+    own_a = jnp.concatenate([qkv_weight[0], attn_out[0], mlp_up[0]], axis=1)
+    allowed, cross_allowed, valid_rows = masks(kept_counts[0], caption_lengths, row_count, decoder)
+    row_weight = jnp.where(decoder, valid_rows, True).astype(f32)[:, None]
+    (
+        full_a, full_d, sum_ca, sum_cd, h1, qkv, mixed, weight, middle, h2, active, slope,
+        gains, layer_out, top, vec,
+    ) = forward(
+        lines, cuts, parts, tokens[0], cotangent[0], allowed.astype(f32), cross_allowed.astype(f32),
+        row_weight, gvec, own_a, mlp_down[0], pack, cross_down,
+    )
+    shard_shapes = [
+        w.shape[-2:]
+        for w in (
+            qkv_weight, attn_out, mlp_up, mlp_down, cross_query, cross_keyval, cross_out, cross_up,
+            cross_down,
+        )
+    ]
+    o_qkv, o_out, o_up, o_d, o_cq, o_ckv, o_co, o_cu, o_cd, input_grad, o_vec = backward(
+        lines, cuts, parts, shard_shapes, tokens[0], top, gains, vec, full_a, full_d, sum_ca,
+        sum_cd, h1, qkv, mixed, weight, middle, h2, active, slope,
+    )
+    g_1, g_2 = (
+        lax.dynamic_slice(o_vec, (2 * tower + i, dp * rows), (1, rows)) for i in range(2)
+    )
+    g_q, g_i, g_c = (
+        lax.dynamic_slice(o_vec, (4 + i, (tower * dp_count + dp) * few), (1, few))[0]
+        for i in range(3)
+    )
+    sums = o_vec[7]
+    encoder_count = jnp.full((4,), float(row_count * dp_count), f32)
+    divisor = jnp.concatenate([encoder_count, jnp.full((6,), 1.0, f32) * sums[10]]) * width
+    rms_values = jnp.sqrt(sums[:10] / divisor)
+    return (
+        layer_out[None], input_grad[None], g_1, o_qkv[None], o_out[None], g_2, o_up[None],
+        o_d[None], g_q, g_i, g_c, o_cq, o_ckv, o_co, o_cu, o_cd, rms_values,
+    )
+
+
+def shards(*arrays):
+    dp_count = lax.axis_size("dp")
+    cross_query, cross_down = arrays[13], arrays[17]
+    fills = dp_count % 4 == 0 and dp_count > 4
+    fills = fills and cross_query.shape[0] % 8 == 0 and cross_down.shape[0] % 16 == 0
+    return fused_shards(*arrays) if fills else plain_shards(*arrays)
 
 
 def solution(mesh):

time: 522 us -> 466 us (0.89); the launches traced: 512 us -> 463 us
  Pallas kernels: 291 us -> 437 us
  waiting for transfers between devices: 95 us -> 0 us
  matrix products: 47.3 us -> 0 us
  local copies, waits for them, and re-layouts: 34.7 us -> 16.4 us
  other arithmetic: 26.7 us -> 9.21 us
  loops' own time: 8.64 us -> 0 us
  starting transfers between devices: 7.03 us -> 0 us
    pallas_call x2, Pallas kernels: 291 us -> 437 us  [the longest x1 238 us: forward(): pl.pallas_call(functools.partial(forward_kernel, lines, cuts, parts), out...]
    ppermute x2 -> x0, waiting for transfers between devices: 95 us -> none  [the longest x1 88.8 us: shards(): returned = lax.ppermute(grad_image, 'tower', [(1, 0)]).astype(f32)]
    dot_general x17 -> x0, matrix products: 44.9 us -> none  [the longest x4 14.6 us: dot_nt(): return jnp.einsum('re,de->rd', a, b, preferred_element_type=jnp.float32)]
    another operation x1 -> x0, loops' own time: 8.64 us -> none  [shards(): lax.cond(decoder, run_cross, skip_cross, (layer_y, arrived))]
    concatenate x3 -> x1, other arithmetic: 10.3 us -> 1.83 us  [fused_shards(): own_a = jnp.concatenate([qkv_weight[0], attn_out[0], mlp_up[0]], axis=1)]
    reshape x2 -> x0, local copies, waits for them, and re-layouts: 7.61 us -> none  [the longest x1 4.92 us: shards(): grad_ca.reshape(2, 2, chips, 2 * few, -1)]
    ppermute x2 -> x0, starting transfers between devices: 7.03 us -> none  [the longest x1 5.74 us: shards(): arrived = lax.ppermute(image_rows, 'tower', [(0, 1)])]
    unnamed x89 -> x41, local copies, waits for them, and re-layouts: 14.2 us -> 9.16 us
  transfers between devices with their start and end apart: 2 -> 0, of which waited for: 2 -> 0; matrix products, arithmetic and copies ran while one was open for 1% -> 0% of each run, Pallas kernels for 0% -> 0%
where the time goes in v2:
time: 466 us; the launch traced here: 463 us
  Pallas kernels  437 us (94%)
  local copies, waits for them, and re-layouts  16.4 us (4%)
  other arithmetic  9.21 us (2%)
    pallas_call x1, Pallas kernels, forward(): pl.pallas_call(functools.partial(forward_kernel, lines, cuts, parts), out...  238 us
    pallas_call x1, Pallas kernels, backward(): pl.pallas_call(functools.partial(backward_kernel, lines, cuts, parts), ou...  199 us

profile of v2, /device:TPU:0, one launch (start us, length us, event | category | flops | bytes accessed | tf_op | source)
XLA Modules:
  0.0 463.4 jit_solution(7646350920264487089)
XLA Ops:
  0.7 0.9 reduce-window.8
  1.6 0.7 select_reduce_fusion
  2.4 0.9 compare_convert_fusion
  3.4 0.7 select_convert_fusion.1.row_weight
  5.6 0.7 tile.63
  6.4 0.7 tile.67
  7.2 0.7 tile.65
  8.6 1.8 pad_maximum_fusion.own_a
  10.6 0.9 maximum_convert_fusion.pack
  11.4 238.0 %shard_map.305 = (bf16[768,6144]{1,0:T(8,128)(2,1)}, bf16[3072,768]{1,0:T(8,128)(2,1)}, bf16[768,3072]{1,0:T(8,128)(2,1)}, bf16[1536,768]{1,0:T(8,128)(2,1)}, bf...) custom-call(bf16[192,768]{1,0:T(8,128)(2,1)} %bitcast.36, ...), custom_call_target="tpu_custom_call" | custom-call | tf_op jit(solution)/shard_map/pallas_call | solution.py:861
  249.4 198.9 %shard_map.306 = (f32[48,2304]{1,0:T(8,128)}, f32[48,768]{1,0:T(8,128)}, f32[48,3072]{1,0:T(8,128)}, f32[192,768]{1,0:T(8,128)}, f32[24,768]{1,0:T(8,128)}, /*in...) custom-call(bf16[192,768]{1,0:T(8,128)(2,1)} %bitcast.37, ...), custom_call_target="tpu_custom_call" | custom-call | tf_op jit(solution)/shard_map/pallas_call | solution.py:1298
  448.3 1.4 fusion.16
  449.7 1.4 dynamic-slice_bitcast_fusion
  451.1 1.3 slice.47
  452.4 1.9 fusion.10
  454.2 0.7 copy.48
  455.0 2.0 copy.49
  456.9 0.8 copy.50
  457.7 0.7 copy.51
  458.4 0.8 copy.52
  459.2 0.8 copy.53
  460.7 0.7 copy.55
  462.0 0.7 copy.57
  462.7 0.7 copy.58
  (56 shorter events, 4.1 us)
Async XLA Ops:
  0.7 8.0 %copy-start.6 = (bf16[1,48,3072]{2,1,0:T(8,128)(2,1)S(1)}, bf16[1,48,3072]{2,1,0:T(8,128)(2,1)}, u32[]{:S(2)}) copy-start(bf16[1,48,3072]{2,1,0:T(8,128)(2,1)} %param.26) | copy-start | bytes 884740
  0.7 9.8 %copy-start.7 = (bf16[24,3072]{1,0:T(8,128)(2,1)S(1)}, bf16[24,3072]{1,0:T(8,128)(2,1)}, u32[]{:S(2)}) copy-start(bf16[24,3072]{1,0:T(8,128)(2,1)} %param.34) | copy-start | bytes 442372
  2.4 8.1 %copy-start.13 = (bf16[24,768]{1,0:T(8,128)(2,1)S(1)}, bf16[24,768]{1,0:T(8,128)(2,1)}, u32[]{:S(2)}) copy-start(bf16[24,768]{1,0:T(8,128)(2,1)} %param.33) | copy-start | bytes 110596
  2.4 8.1 %copy-start.10 = (bf16[24,1536]{1,0:T(8,128)(2,1)S(1)}, bf16[24,1536]{1,0:T(8,128)(2,1)}, u32[]{:S(2)}) copy-start(bf16[24,1536]{1,0:T(8,128)(2,1)} %param.32) | copy-start | bytes 221188
  3.3 7.2 %copy-start.14 = (bf16[24,768]{1,0:T(8,128)(2,1)S(1)}, bf16[24,768]{1,0:T(8,128)(2,1)}, u32[]{:S(2)}) copy-start(bf16[24,768]{1,0:T(8,128)(2,1)} %param.31) | copy-start | bytes 110596
  249.4 204.8 %copy-start.4 = (bf16[192,768]{1,0:T(8,128)(2,1)S(1)}, bf16[192,768]{1,0:T(8,128)(2,1)}, u32[]{:S(2)}) copy-start(bf16[192,768]{1,0:T(8,128)(2,1)} %get-tuple-element.44) | copy-start | bytes 884740
  448.3 8.6 %copy-start.2 = (f32[48,2304]{1,0:T(8,128)S(1)}, f32[48,2304]{1,0:T(8,128)}, u32[]{:S(2)}) copy-start(f32[48,2304]{1,0:T(8,128)} %get-tuple-element.62) | copy-start | bytes 1327108
  454.2 3.5 copy-start.9
  455.0 3.4 copy-start.1
  456.9 2.3 copy-start
  458.4 1.7 copy-start.12
  458.4 2.3 copy-start.8
  458.4 3.0 copy-start.11
  458.4 3.6 copy-start.5
  459.2 3.5 copy-start.3
